TPU v7x, 32 devices: a whole 2x2x4 slice. The times are simulated.
32 devices in a mesh: seq: 8 (over z, x), mp: 4 (over y, core).
Axes of the slice: x: 2, y: 2, z: 4, core: 2. Of those that a mesh axis runs over, the one named last changes fastest.
Arguments:
- hidden: bfloat16 [4096, 4096], P('seq', 'mp'), may hold values from -6 to 6
- w_zx: bfloat16 [4096, 2, 4096], P(None, None, 'mp'), may hold values from -0.09375 to 0.09375
- w_bc: bfloat16 [4096, 2, 512], P(None, None, 'mp'), may hold values from -0.09375 to 0.09375
- w_dt: bfloat16 [4096, 64], P(None, 'mp'), may hold values from -0.09375 to 0.09375
- conv_x: float32 [4, 4096], P(None, 'mp'), may hold values from -3 to 3
- conv_x_bias: float32 [4096], P('mp'), may hold values from -3 to 3
- conv_bc: float32 [4, 2, 512], P(None, None, 'mp'), may hold values from -3 to 3
- conv_bc_bias: float32 [2, 512], P(None, 'mp'), may hold values from -3 to 3
- a_log: float32 [64], P('mp'), may hold values from -9.5 to -0.5
- dt_bias: float32 [64], P('mp'), may hold values from -4 to -1
- d_skip: float32 [64], P('mp'), may hold values from 0.5 to 4
- norm_gain: float32 [4096], P('mp'), may hold values from 0.4 to 1.6
- state_bank: float32 [2, 64, 64, 128], P(None, 'mp'), may hold values from -2 to 2
- conv_bank_x: bfloat16 [2, 3, 4096], P(None, None, 'mp'), may hold values from -5 to 5
- conv_bank_bc: bfloat16 [2, 3, 2, 512], P(None, None, None, 'mp'), may hold values from -5 to 5
- prompt_blocks: int32 [3], replicated, may hold values from 1 to 12, 16 in all
- prompt_order: int32 [3], replicated, may hold values from 0 to 2, each once
- resume_slot: int32 [3], replicated, may hold values from 0 to 2
Outputs:
- mixed: bfloat16 [4096, 4096], P('seq', 'mp')
Inputs may be any that keep to these rules, and one draw needn't show every extreme that they name: `prompt_blocks`: blocks of each prompt; they sum to 16 and the longest is exactly 12. `prompt_order`: A permutation of the prompts. `resume_slot`: 2 means a fresh start from zero state and zero convolution rows.
All inputs are finite; a program needn't handle non-finite values.
Results may differ from a plain program's by a relative error of at most 0.0068.
Values may be sent and summed in bfloat16 or wider, within the bound.
A program may use at most 192 MiB of HBM per device.

v0:
```python
import jax
import jax.numpy as jnp
from jax import lax
from jax.sharding import PartitionSpec as P

WIDTH = 4096
HEAD_DIM = 64
STATE = 128
BLOCK = 256
KERNEL = 4
BANK = 2


def from_behind(value, axis, steps):
    count = lax.axis_size(axis)
    pairs = [(source, (source + steps) % count) for source in range(count)]
    return lax.ppermute(value, axis, pairs)


def entering(value, axis, join, neutral):
    count, mine = (lax.axis_size(axis), lax.axis_index(axis))
    pieces = jax.tree.map(lambda part: lax.all_gather(part, axis), value)
    total = jax.tree.map(
        lambda part, zero: jnp.full_like(part, 0) + jnp.asarray(zero, part.dtype), value, neutral
    )

    def turn(position, total):
        longer = join(total, jax.tree.map(lambda part: part[position], pieces))
        return jax.tree.map(lambda new, old: jnp.where(position < mine, new, old), longer, total)

    return lax.fori_loop(0, count - 1, turn, total)


def broadcast(block, axis, source):
    block = jnp.where(lax.axis_index(axis) == source, block, jnp.zeros_like(block))
    return lax.psum(block, axis)


def combine(earlier, later):
    return (earlier[0] * later[0], later[0][..., None, None] * earlier[1] + later[1])


def per_device(
    hidden,
    w_zx,
    w_bc,
    w_dt,
    conv_x,
    conv_x_bias,
    conv_bc,
    conv_bc_bias,
    a_log,
    dt_bias,
    d_skip,
    norm_gain,
    state_bank,
    conv_bank_x,
    conv_bank_bc,
    prompt_blocks,
    prompt_order,
    resume_slot,
):
    devices = lax.axis_size("seq")
    place = lax.axis_index("seq")
    rows_dev = hidden.shape[0]
    blocks = rows_dev // BLOCK
    inner_dev = w_zx.shape[2]
    gstate_dev = w_bc.shape[2]
    heads_dev = w_dt.shape[1]
    groups_dev = gstate_dev // STATE
    per_group = heads_dev // groups_dev
    channels = inner_dev + 2 * gstate_dev
    prompts = prompt_blocks.shape[0]
    flat_zx = w_zx.reshape(WIDTH, 2 * inner_dev)
    flat_bc = w_bc.reshape(WIDTH, 2 * gstate_dev)
    piece = lax.all_gather(hidden, "mp", axis=1, tiled=True)
    zx_sum = jnp.dot(piece, flat_zx, preferred_element_type=jnp.float32)
    bc_sum = jnp.dot(piece, flat_bc, preferred_element_type=jnp.float32)
    dt_raw = jnp.dot(piece, w_dt, preferred_element_type=jnp.float32)
    zx = zx_sum.astype(jnp.bfloat16)
    bc = bc_sum.astype(jnp.bfloat16)
    gate = zx[:, :inner_dev]
    mixin = jnp.concatenate([zx[:, inner_dev:], bc], axis=1).reshape(blocks, BLOCK, channels)
    own_tails = mixin[:, BLOCK - (KERNEL - 1) :, :]
    arrived = from_behind(own_tails, "seq", 1)
    wrapped = jnp.concatenate([jnp.zeros_like(arrived[:1]), arrived[:-1]], axis=0)
    before = jnp.where(place > 0, arrived, wrapped)
    prompt_ids = jnp.arange(prompts, dtype=jnp.int32)
    order_hot = (prompt_order[:, None] == prompt_ids[None, :]).astype(jnp.int32)
    lengths = jnp.sum(order_hot * prompt_blocks[None, :], axis=1)
    slots = jnp.sum(order_hot * resume_slot[None, :], axis=1)
    ends = jnp.cumsum(lengths)
    starts = ends - lengths
    stream_ids = jnp.arange(blocks, dtype=jnp.int32) * devices + place
    inside = (
        (stream_ids[:, None] >= starts[None, :]) & (stream_ids[:, None] < ends[None, :])
    ).astype(jnp.int32)
    block_slot = jnp.sum(inside * slots[None, :], axis=1)
    first = jnp.any(stream_ids[:, None] == starts[None, :], axis=1)
    pick = (block_slot[:, None] == jnp.arange(BANK, dtype=jnp.int32)[None, :]).astype(jnp.float32)
    bank_state = jnp.einsum("cr,rhpn->chpn", pick, state_bank, precision=lax.Precision.HIGHEST)
    bank_rows = jnp.concatenate(
        [conv_bank_x, conv_bank_bc.reshape(BANK, KERNEL - 1, 2 * gstate_dev)], axis=2
    )
    bank_tail = jnp.einsum("cr,rkz->ckz", pick, bank_rows.astype(jnp.float32)).astype(jnp.bfloat16)
    tail = jnp.where(first[:, None, None], bank_tail, before)
    kernel = jnp.concatenate([conv_x, conv_bc.reshape(KERNEL, 2 * gstate_dev)], axis=1)
    bias = jnp.concatenate([conv_x_bias, conv_bc_bias.reshape(2 * gstate_dev)], axis=0)
    padded = jnp.concatenate([tail, mixin], axis=1).astype(jnp.float32)
    acc = bias[None, None, :] + padded[:, 0:BLOCK] * kernel[0]
    for k in range(1, KERNEL):
        acc = acc + padded[:, k : k + BLOCK] * kernel[k]
    conv = jax.nn.silu(acc).astype(jnp.bfloat16)
    xs = conv[..., :inner_dev].reshape(blocks, BLOCK, groups_dev, per_group, HEAD_DIM)
    bs = conv[..., inner_dev : inner_dev + gstate_dev].reshape(blocks, BLOCK, groups_dev, STATE)
    cq = conv[..., inner_dev + gstate_dev :].reshape(blocks, BLOCK, groups_dev, STATE)
    dt = jax.nn.softplus(dt_raw.reshape(blocks, BLOCK, heads_dev) + dt_bias[None, None, :])
    cum = jnp.cumsum(dt * (-jnp.exp(a_log))[None, None, :], axis=1)
    scores = jnp.einsum("cqgn,ckgn->cgqk", cq, bs, preferred_element_type=jnp.float32)
    cum_h = cum.transpose(0, 2, 1)
    lower = jnp.arange(BLOCK)[:, None] >= jnp.arange(BLOCK)[None, :]
    damp = jnp.exp(
        jnp.where(lower[None, None], cum_h[:, :, :, None] - cum_h[:, :, None, :], -jnp.inf)
    )
    damp = damp.reshape(blocks, groups_dev, per_group, BLOCK, BLOCK)
    dt_h = dt.transpose(0, 2, 1).reshape(blocks, groups_dev, per_group, 1, BLOCK)
    mix = (scores[:, :, None] * damp * dt_h).astype(jnp.bfloat16)
    y_intra = jnp.einsum("cgjqk,ckgjp->cqgjp", mix, xs, preferred_element_type=jnp.float32)
    last = cum[:, -1, :]
    grow = jnp.exp(last)
    factor = (dt * jnp.exp(last[:, None, :] - cum)).reshape(blocks, BLOCK, groups_dev, per_group, 1)
    weighted = (xs.astype(jnp.float32) * factor).astype(jnp.bfloat16)
    local_state = jnp.einsum(
        "cqgjp,cqgn->cgjpn", weighted, bs, preferred_element_type=jnp.float32
    ).reshape(blocks, heads_dev, HEAD_DIM, STATE)
    step_a = jnp.where(first[:, None], 0.0, grow)
    step_b = local_state + jnp.where(
        first[:, None, None, None], grow[:, :, None, None] * bank_state, 0.0
    )
    carry = jnp.zeros((heads_dev, HEAD_DIM, STATE), jnp.float32)
    found = []
    for row in range(blocks):
        own = (step_a[row], step_b[row])
        unit = (jnp.ones_like(own[0]), jnp.zeros_like(own[1]))
        prior_a, prior_b = entering(own, "seq", combine, unit)
        found.append(prior_a[:, None, None] * carry + prior_b)
        whole_a, whole_b = combine((prior_a, prior_b), own)
        carry = broadcast(whole_a[:, None, None] * carry + whole_b, "seq", devices - 1)
    previous = jnp.stack(found, axis=0)
    state_in = jnp.where(first[:, None, None, None], bank_state, previous)
    read = jnp.einsum(
        "cqgn,cgjpn->cqgjp",
        cq.astype(jnp.float32),
        state_in.reshape(blocks, groups_dev, per_group, HEAD_DIM, STATE),
        precision=lax.Precision.HIGHEST,
    )
    growth = jnp.exp(cum).reshape(blocks, BLOCK, groups_dev, per_group, 1)
    skip = d_skip.reshape(1, 1, groups_dev, per_group, 1)
    y_total = y_intra + growth * read + skip * xs.astype(jnp.float32)
    gated = y_total.reshape(rows_dev, inner_dev) * jax.nn.silu(gate.astype(jnp.float32))
    grouped = gated.reshape(rows_dev, groups_dev, inner_dev // groups_dev)
    scale = lax.rsqrt(jnp.mean(grouped * grouped, axis=2, keepdims=True) + 1e-05)
    result = (grouped * scale).reshape(rows_dev, inner_dev) * norm_gain[None, :]
    return result.astype(jnp.bfloat16)


def solution(mesh):
    placed = (
        P("seq", "mp"),
        P(None, None, "mp"),
        P(None, None, "mp"),
        P(None, "mp"),
        P(None, "mp"),
        P("mp"),
        P(None, None, "mp"),
        P(None, "mp"),
        P("mp"),
        P("mp"),
        P("mp"),
        P("mp"),
        P(None, "mp", None, None),
        P(None, None, "mp"),
        P(None, None, None, "mp"),
        P(),
        P(),
        P(),
    )
    return jax.shard_map(
        per_device, mesh=mesh, in_specs=placed, out_specs=P("seq", "mp"), check_vma=False
    )
```

profile of v0, /device:TPU:0, one launch (start us, length us, event | category | flops | bytes accessed | tf_op | source)
XLA Modules:
  0.0 325.0 jit_solution(3045389441153391133)
XLA Ops:
  7.4 17.3 %copy.108 = bf16[512,8,2,1024]{3,1,2,0:T(8,128)(2,1)} copy(bf16[512,8,2,1024]{3,2,1,0:T(2,128)(2,1)} %bitcast.135) | data formatting | bytes 33554432
  26.2 2.5 fusion.29
  28.7 17.4 %all-gather.6.cloned.1.call-done = bf16[512,4096]{1,0:T(8,128)(2,1)} async-done(((bf16[512,1024]{1,0:T(8,128)(2,1)}), bf16[512,4096]{1,0:T(8,128)(2,1)}) %all-gather.6.cloned.1.call-update) | async-done | bytes 4194320 | tf_op jit(solution)/shard_map/all_gather | solution.py:76
  46.1 15.7 %convolution_convert_fusion = bf16[512,2048]{1,0:T(8,128)(2,1)S(1)} fusion(bf16[512,4096]{1,0:T(8,128)(2,1)} %all-gather.6.cloned.1.call-done, bf16[4096,2048]{1,0:T(8,128)(2,1)} %bitcast.136), kind=kOutput, calls=%fused_computation.18 | convolution fusion | flops 8590983168 | bytes 23068672 | tf_op jit(solution)/shard_map/dot_general | solution.py:77
  62.0 2.2 copy-done.27
  64.3 1.3 fusion.22
  65.8 1.7 collective-permute-start
  67.5 1.2 fusion.54
  72.9 1.7 multiply_convert_fusion.2
  75.8 1.7 slice_convert_fusion
  78.0 1.5 convolution_add_fusion
  81.5 18.8 %all-gather = f32[8,1,16]{2,1,0:T(1,128)S(1)} all-gather(f32[1,1,16]{2,1,0:T(1,128)S(1)} %get-tuple-element.318), channel_id=1, replica_groups=mesh['seq'=8,'mp'=4] {'seq'}, dimensions={0}, use_global_device_ids=true | all-gather | bytes 576 | tf_op jit(solution)/shard_map/all_gather | solution.py:22
  100.4 16.2 %all-gather.1 = f32[8,1,16]{2,1,0:T(1,128)S(1)} all-gather(f32[1,1,16]{2,1,0:T(1,128)S(1)} %get-tuple-element.317), channel_id=1, replica_groups=mesh['seq'=8,'mp'=4] {'seq'}, dimensions={0}, use_global_device_ids=true | all-gather | bytes 576 | tf_op jit(solution)/shard_map/all_gather | solution.py:22
  116.6 2.9 copy.95
  119.5 2.0 fusion.36
  121.5 31.0 %all-gather.8.cloned.1.call-done = f32[8,16,64,128]{3,2,1,0:T(8,128)} async-done(((f32[1,16,64,128]{3,2,1,0:T(8,128)}), f32[8,16,64,128]{3,2,1,0:T(8,128)}) %all-gather.8.cloned.1.call-update) | async-done | bytes 4194320 | tf_op jit(solution)/shard_map/all_gather | solution.py:22
  152.5 8.5 %while.32 = (s32[]{:T(128)}, f32[16]{0:T(128)S(1)}, f32[16,64,128]{2,1,0:T(8,128)S(1)}, s32[]{:T(128)}, f32[8,16]{1,0:T(8,128)S(1)}, /*index=5*/f32[8,16,64,128]{3,2,1,0:T(8,128)}, s32[]{:T(128)}, s32[]{:T(128)}) while((s32[]{:T(128)}, f32[16]{0:T(128)S(1)}, f32[16,64,128]{2,1,0:T(8,128)S(1)}, s32[]{:T(128)}, ...), condition=%wide.region_8.9_spmd.clone, body=%wide.region_7.8_spmd.clone.sunk | while | flops 524340 | bytes 1573299 | solution.py:31
  153.8 1.2 fusion.63
  157.4 1.2 fusion.63
  159.9 1.2 fusion.63
  162.3 64.1 %all-gather.10.cloned.1.call-done = f32[8,16,64,128]{3,2,1,0:T(8,128)} async-done(((f32[1,16,64,128]{3,2,1,0:T(8,128)}), f32[8,16,64,128]{3,2,1,0:T(8,128)}) %all-gather.10.cloned.1.call-update) | async-done | bytes 4194320 | tf_op jit(solution)/shard_map/all_gather | solution.py:22
  226.4 8.6 %while.33 = (s32[]{:T(128)}, f32[16]{0:T(128)S(1)}, f32[16,64,128]{2,1,0:T(8,128)S(1)}, s32[]{:T(128)}, f32[8,16]{1,0:T(8,128)S(1)}, /*index=5*/f32[8,16,64,128]{3,2,1,0:T(8,128)}, s32[]{:T(128)}, s32[]{:T(128)}) while((s32[]{:T(128)}, f32[16]{0:T(128)S(1)}, f32[16,64,128]{2,1,0:T(8,128)S(1)}, s32[]{:T(128)}, ...), condition=%wide.region_10.11_spmd.clone, body=%wide.region_9.10_spmd.clone.sunk | while | flops 524340 | bytes 1573299 | solution.py:31
  226.4 1.2 fusion.64
  232.5 1.2 fusion.64
  233.8 1.2 fusion.64
  235.0 65.3 %all-reduce.3.cloned.1.call-done = f32[16,64,128]{2,1,0:T(8,128)} async-done(((f32[16,64,128]{2,1,0:T(8,128)}), f32[16,64,128]{2,1,0:T(8,128)}) %all-reduce.3.cloned.1.call-update) | async-done | bytes 524304 | tf_op jit(solution)/shard_map/psum | solution.py:36
  302.6 2.1 fusion.25
  304.8 2.6 fusion.21
  307.4 3.8 %copy.102 = f32[2,256,1,16,64]{4,3,1,0,2:T(8,128)} copy(f32[2,256,1,16,64]{1,4,3,0,2:T(8,128)S(1)} %fusion.21) | data formatting | bytes 4194304 | tf_op jit(solution)/shard_map/reshape | solution.py:160
  311.2 3.5 %reshape.236 = f32[512,1024]{1,0:T(8,128)S(1)} reshape(f32[2,256,1,16,64]{4,3,1,0,2:T(8,128)} %copy.102) | data formatting | bytes 4194304 | tf_op jit(solution)/shard_map/reshape | solution.py:160
  314.7 2.1 multiply_reduce_fusion
  316.8 1.7 multiply_convert_fusion.3
  (134 shorter events, 23.4 us)
Async XLA Ops:
  6.5 19.7 %copy-start = (f32[2,16,64,128]{3,2,1,0:T(8,128)S(1)}, f32[2,16,64,128]{3,2,1,0:T(8,128)}, u32[]{:S(2)}) copy-start(f32[2,16,64,128]{3,2,1,0:T(8,128)} %param.34) | copy-start | bytes 3145732
  6.5 39.6 %all-gather.6.cloned.1.call-start = ((), (), s32[]{:S(2)}) async-start(), calls=%async_computation | async-start | bytes 5242880 | tf_op jit(solution)/shard_map/all_gather | solution.py:76
  7.3 145.3 %all-gather.8.cloned.1.call-start = ((), (), s32[]{:S(2)}) async-start(), calls=%async_computation.1 | async-start | bytes 4718592 | tf_op jit(solution)/shard_map/all_gather | solution.py:22
  7.3 17.4 %copy-start.24 = (s32[3]{0:T(128)S(1)}, s32[3]{0:T(128)}, u32[]{:S(2)}) copy-start(s32[3]{0:T(128)} %param.37) | copy-start | bytes 40
  7.3 17.4 %copy-start.25 = (s32[3]{0:T(128)S(1)}, s32[3]{0:T(128)}, u32[]{:S(2)}) copy-start(s32[3]{0:T(128)} %param.38) | copy-start | bytes 40
  7.3 17.3 %copy-start.26 = (s32[3]{0:T(128)S(1)}, s32[3]{0:T(128)}, u32[]{:S(2)}) copy-start(s32[3]{0:T(128)} %param.39) | copy-start | bytes 40
  7.3 17.7 %copy-start.18 = (bf16[2,3,2,128]{3,2,1,0:T(2,128)(2,1)S(1)}, bf16[2,3,2,128]{3,2,1,0:T(2,128)(2,1)}, u32[]{:S(2)}) copy-start(bf16[2,3,2,128]{3,2,1,0:T(2,128)(2,1)} %param.36) | copy-start | bytes 9220
  7.3 18.3 %copy-start.16 = (f32[1024]{0:T(1024)S(1)}, f32[1024]{0:T(1024)}, u32[]{:S(2)}) copy-start(f32[1024]{0:T(1024)} %param.27) | copy-start | bytes 12292
  7.4 18.3 %copy-start.23 = (f32[2,128]{1,0:T(2,128)S(1)}, f32[2,128]{1,0:T(2,128)}, u32[]{:S(2)}) copy-start(f32[2,128]{1,0:T(2,128)} %param.29) | copy-start | bytes 3076
  7.4 18.3 %copy-start.13 = (f32[4,1024]{1,0:T(4,128)S(1)}, f32[4,1024]{1,0:T(4,128)}, u32[]{:S(2)}) copy-start(f32[4,1024]{1,0:T(4,128)} %param.26) | copy-start | bytes 49156
  7.4 18.7 %copy-start.17 = (f32[4,2,128]{2,1,0:T(2,128)S(1)}, f32[4,2,128]{2,1,0:T(2,128)}, u32[]{:S(2)}) copy-start(f32[4,2,128]{2,1,0:T(2,128)} %param.28) | copy-start | bytes 12292
  7.4 18.8 %copy-start.29 = (f32[16]{0:T(128)S(1)}, f32[16]{0:T(128)}, u32[]{:S(2)}) copy-start(f32[16]{0:T(128)} %param.30) | copy-start | bytes 196
  26.1 35.8 %copy-start.21 = (s32[2]{0:T(128)}, s32[2]{0:T(128)S(1)}, u32[]{:S(2)}) copy-start(s32[2]{0:T(128)S(1)} %fusion.45) | copy-start | bytes 28
  46.1 15.9 %copy-start.5 = (bf16[512,4096]{1,0:T(8,128)(2,1)S(1)}, bf16[512,4096]{1,0:T(8,128)(2,1)}, u32[]{:S(2)}) copy-start(bf16[512,4096]{1,0:T(8,128)(2,1)} %all-gather.6.cloned.1.call-done) | copy-start | bytes 12582916
  61.9 3.7 %copy-start.3 = (bf16[512,2048]{1,0:T(8,128)(2,1)}, bf16[512,2048]{1,0:T(8,128)(2,1)S(1)}, u32[]{:S(2)}) copy-start(bf16[512,2048]{1,0:T(8,128)(2,1)S(1)} %convolution_convert_fusion) | copy-start | bytes 6291460
  61.9 2.4 copy-start.27
  65.7 2.9 copy-start.20
  65.7 6.7 %copy-start.19 = (bf16[2,3,256]{2,0,1:T(2,128)(2,1)S(1)}, bf16[2,3,256]{2,0,1:T(2,128)(2,1)}, u32[]{:S(2)}) copy-start(bf16[2,3,256]{2,0,1:T(2,128)(2,1)} %reshape.217) | copy-start | bytes 9220
  65.7 6.7 %copy-start.22 = (s32[2]{0:T(128)S(1)}, s32[2]{0:T(128)}, u32[]{:S(2)}) copy-start(s32[2]{0:T(128)} %copy-done.21) | copy-start | bytes 28
  65.7 6.7 %copy-start.28 = (bf16[2,3,1024]{2,0,1:T(2,128)(2,1)S(1)}, bf16[2,3,1024]{2,0,1:T(2,128)(2,1)}, u32[]{:S(2)}) copy-start(bf16[2,3,1024]{2,0,1:T(2,128)(2,1)} %param.35) | copy-start | bytes 36868
  65.8 6.7 %collective-permute-start = (bf16[2,3,1280]{2,0,1:T(2,128)(2,1)S(1)}, bf16[2,3,1280]{2,0,1:T(2,128)(2,1)S(1)}, u32[]{:S(2)}, u32[]{:S(2)}) collective-permute-start(bf16[2,3,1280]{2,0,1:T(2,128)(2,1)S(1)} %copy.104), channel_id=1, source_target_pairs={{0,4},{4,8},{8,12},{12,16},{16,20},{20,24},{24,28},{28,0},{1,5},{5... | collective-permute-start | bytes 46088 | tf_op jit(solution)/shard_map/ppermute | solution.py:17
  77.9 2.7 copy-start.6
  80.7 145.7 %all-gather.10.cloned.1.call-start = ((), (), s32[]{:S(2)}) async-start(), calls=%async_computation.2 | async-start | bytes 4718592 | tf_op jit(solution)/shard_map/all_gather | solution.py:22
  81.4 218.9 %all-reduce.3.cloned.1.call-start = ((), (), s32[]{:S(2)}) async-start(), calls=%async_computation.3 | async-start | bytes 1048576 | tf_op jit(solution)/shard_map/psum | solution.py:36
  226.4 75.1 %copy-start.9 = (f32[16,64,128]{2,1,0:T(8,128)S(1)}, f32[16,64,128]{2,1,0:T(8,128)}, u32[]{:S(2)}) copy-start(f32[16,64,128]{2,1,0:T(8,128)} %get-tuple-element.309) | copy-start | bytes 1572868
  301.4 3.3 %copy-start.10 = (f32[2,256,256]{2,1,0:T(8,128)S(1)}, f32[2,256,256]{2,1,0:T(8,128)}, u32[]{:S(2)}) copy-start(f32[2,256,256]{2,1,0:T(8,128)} %fusion.36) | copy-start | bytes 1572868
  302.6 2.1 copy-start.7
  302.6 2.1 copy-start.8
  302.6 2.1 copy-start.12
  302.6 2.1 copy-start.30
  314.7 2.1 copy-start.4
  314.7 2.1 copy-start.14
  (4 other events, 5.3 us)
Sparse Core Ops, SparseCore 0:
  8.9 37.1 all-gather.5
  80.8 71.7 all-gather.7
  154.7 71.6 all-gather.9
  229.6 70.5 all-reduce.2
where the time goes:
time: 326 us; the launch traced here: 325 us
  waiting for transfers between devices  180 us (55%)
  blocking collectives  35 us (11%)
  local copies, waits for them, and re-layouts  33.7 us (10%)
  other arithmetic  31.2 us (10%)
  matrix products  29.2 us (9%)
  between operations  13.7 us (4%)
    all_gather x2, waiting for transfers between devices, entering(): pieces = jax.tree.map(lambda part: lax.all_gather(part, axis), value)  95.1 us
    psum x1, waiting for transfers between devices, broadcast(): return lax.psum(block, axis)  65.3 us
    all_gather x2, blocking collectives, entering(): pieces = jax.tree.map(lambda part: lax.all_gather(part, axis), value)  35 us
    unnamed x66, local copies, waits for them, and re-layouts  20.8 us
    all_gather x1, waiting for transfers between devices, per_device(): piece = lax.all_gather(hidden, 'mp', axis=1, tiled=True)  17.4 us
    select_n x28, other arithmetic, turn(): jnp.where(position < mine, new, old)  16.8 us
    dot_general x1, matrix products, per_device(): zx_sum = jnp.dot(piece, flat_zx, preferred_element_type=jnp.float32)  15.7 us
    reshape x2, local copies, waits for them, and re-layouts, per_device(): y_total.reshape(rows_dev, inner_dev) * jax.nn.silu(gate.astype(jnp.float32))  7.27 us
  transfers between devices with their start and end apart: 5, of which 5 were waited for; matrix products, arithmetic and copies ran while one was open for 15% of the time, Pallas kernels for 0%

commit v1 on v0

--- a/solution.py
+++ b/solution.py
@@ -1,6 +1,10 @@
+import functools
+
 import jax
 import jax.numpy as jnp
 from jax import lax
+from jax.experimental import pallas as pl
+from jax.experimental.pallas import tpu as pltpu
 from jax.sharding import PartitionSpec as P
 
 WIDTH = 4096
@@ -17,27 +21,123 @@
     return lax.ppermute(value, axis, pairs)
 
 
-def entering(value, axis, join, neutral):
-    count, mine = (lax.axis_size(axis), lax.axis_index(axis))
-    pieces = jax.tree.map(lambda part: lax.all_gather(part, axis), value)
-    total = jax.tree.map(
-        lambda part, zero: jnp.full_like(part, 0) + jnp.asarray(zero, part.dtype), value, neutral
-    )
-
-    def turn(position, total):
-        longer = join(total, jax.tree.map(lambda part: part[position], pieces))
-        return jax.tree.map(lambda new, old: jnp.where(position < mine, new, old), longer, total)
-
-    return lax.fori_loop(0, count - 1, turn, total)
-
-
-def broadcast(block, axis, source):
-    block = jnp.where(lax.axis_index(axis) == source, block, jnp.zeros_like(block))
-    return lax.psum(block, axis)
-
-
-def combine(earlier, later):
-    return (earlier[0] * later[0], later[0][..., None, None] * earlier[1] + later[1])
+def exchange_kernel(
+    count, blocks, local_ref, grow_ref, pick_ref, bank_ref, out_ref,
+    got, back, grown, send_a, recv_a, send_g, recv_g, send_b, recv_b,
+):
+    me = lax.axis_index("seq")
+    barrier = pltpu.get_barrier_semaphore()
+    for k in range(1, count):
+        pl.semaphore_signal(
+            barrier,
+            inc=1,
+            device_id={"seq": lax.rem(me + k, count)},
+            device_id_type=pl.DeviceIdType.MESH,
+        )
+    pl.semaphore_wait(barrier, count - 1)
+    outward = []
+    for k in range(1, count):
+        peer = lax.rem(me + k, count)
+        for src, dst, send, recv in (
+            (grow_ref, grown, send_g, recv_g),
+            (local_ref, got, send_a, recv_a),
+        ):
+            copy = pltpu.make_async_remote_copy(
+                src_ref=src.at[peer],
+                dst_ref=dst.at[me],
+                send_sem=send.at[k - 1],
+                recv_sem=recv.at[k - 1],
+                device_id={"seq": peer},
+                device_id_type=pl.DeviceIdType.MESH,
+            )
+            copy.start()
+            outward.append(copy)
+    got[me] = local_ref[me]
+    grown[me] = grow_ref[me]
+    for copy in outward:
+        copy.wait()
+    rows = local_ref.shape[2]
+    parts = max(rows // HEAD_DIM, 1)
+    span = rows // parts
+    for part in range(parts):
+        here = slice(part * span, (part + 1) * span)
+        state = jnp.zeros((span, STATE), jnp.float32)
+        for c in range(count * blocks):
+            device, row = c % count, c // count
+            state = pick_ref[c, 0:1, :] * state
+            for r in range(BANK):
+                state = state + pick_ref[c, 1 + r : 2 + r, :] * bank_ref[r, here, :]
+            back[device, row, here, :] = state.astype(jnp.bfloat16)
+            at = row * parts + part
+            state = grown[device, at : at + 1, :] * state + got[device, row, here, :].astype(
+                jnp.float32
+            )
+    homeward = []
+    for k in range(1, count):
+        peer = lax.rem(me + k, count)
+        copy = pltpu.make_async_remote_copy(
+            src_ref=back.at[peer],
+            dst_ref=out_ref.at[me],
+            send_sem=send_b.at[k - 1],
+            recv_sem=recv_b.at[k - 1],
+            device_id={"seq": peer},
+            device_id_type=pl.DeviceIdType.MESH,
+        )
+        copy.start()
+        homeward.append(copy)
+    out_ref[me] = back[me]
+    for copy in homeward:
+        copy.wait()
+
+
+def entering_states(local_state, grow, pick, first, bank, place, count):
+    blocks, rows_all, _ = local_state.shape
+    heads = grow.shape[1]
+    rows = rows_all // count
+    local = local_state.astype(jnp.bfloat16).reshape(blocks, count, rows, STATE)
+    local = local.transpose(1, 0, 2, 3)
+    if heads < count:
+        grow = jnp.repeat(grow, count // heads, axis=1)
+    grow = grow.reshape(blocks, count, -1).transpose(1, 0, 2).reshape(count, -1)
+    padded = -(-grow.shape[1] // 8) * 8
+    grow = jnp.pad(grow, ((0, 0), (0, padded - grow.shape[1])))
+    grow = jnp.broadcast_to(grow[:, :, None], (count, padded, STATE))
+    picks = jnp.concatenate([1.0 - first[:, None], first[:, None] * pick], axis=1)
+    picks = jnp.pad(picks, ((0, 0), (0, 8 - picks.shape[1])))
+    picks = jnp.broadcast_to(picks[:, :, None], (count * blocks, 8, STATE))
+    mine = lax.dynamic_slice_in_dim(bank, place * rows, rows, axis=1)
+    dma = pltpu.SemaphoreType.DMA((count - 1,))
+    out = pl.pallas_call(
+        functools.partial(exchange_kernel, count, blocks),
+        out_shape=jax.ShapeDtypeStruct((count, blocks, rows, STATE), jnp.bfloat16),
+        in_specs=[pl.BlockSpec(memory_space=pltpu.VMEM)] * 4,
+        out_specs=pl.BlockSpec(memory_space=pltpu.VMEM),
+        scratch_shapes=[
+            pltpu.VMEM((count, blocks, rows, STATE), jnp.bfloat16),
+            pltpu.VMEM((count, blocks, rows, STATE), jnp.bfloat16),
+            pltpu.VMEM((count, padded, STATE), jnp.float32),
+            dma, dma, dma, dma, dma, dma,
+        ],
+        compiler_params=pltpu.CompilerParams(collective_id=0, has_side_effects=True),
+        name="exchange",
+    )(local, grow, picks, mine)
+    return out.transpose(1, 0, 2, 3).reshape(blocks, rows_all, STATE)
+
+
+def swap(value, axis, bit):
+    count = lax.axis_size(axis)
+    return lax.ppermute(value, axis, [(source, source ^ bit) for source in range(count)])
+
+
+def gather_columns(rows, axis):
+    mine, width = lax.axis_index(axis), rows.shape[1]
+    far = swap(rows, axis, 2)
+    near = swap(rows, axis, 1)
+    both = swap(far, axis, 1)
+    whole = jnp.zeros((rows.shape[0], width * 4), rows.dtype)
+    for bits, part in ((0, rows), (1, near), (2, far), (3, both)):
+        whole = lax.dynamic_update_slice_in_dim(whole, part, (mine ^ bits) * width, axis=1)
+    return whole
 
 
 def per_device(
@@ -73,12 +173,15 @@
     prompts = prompt_blocks.shape[0]
     flat_zx = w_zx.reshape(WIDTH, 2 * inner_dev)
     flat_bc = w_bc.reshape(WIDTH, 2 * gstate_dev)
-    piece = lax.all_gather(hidden, "mp", axis=1, tiled=True)
-    zx_sum = jnp.dot(piece, flat_zx, preferred_element_type=jnp.float32)
-    bc_sum = jnp.dot(piece, flat_bc, preferred_element_type=jnp.float32)
-    dt_raw = jnp.dot(piece, w_dt, preferred_element_type=jnp.float32)
-    zx = zx_sum.astype(jnp.bfloat16)
-    bc = bc_sum.astype(jnp.bfloat16)
+    pieces = []
+    for row in range(blocks):
+        pieces.append(gather_columns(hidden[row * BLOCK : (row + 1) * BLOCK], "mp"))
+    zx, bc, dt_raw = [], [], []
+    for piece in pieces:
+        zx.append(jnp.dot(piece, flat_zx, preferred_element_type=jnp.float32).astype(jnp.bfloat16))
+        bc.append(jnp.dot(piece, flat_bc, preferred_element_type=jnp.float32).astype(jnp.bfloat16))
+        dt_raw.append(jnp.dot(piece, w_dt, preferred_element_type=jnp.float32))
+    zx, bc, dt_raw = (jnp.concatenate(parts, axis=0) for parts in (zx, bc, dt_raw))
     gate = zx[:, :inner_dev]
     mixin = jnp.concatenate([zx[:, inner_dev:], bc], axis=1).reshape(blocks, BLOCK, channels)
     own_tails = mixin[:, BLOCK - (KERNEL - 1) :, :]
@@ -91,14 +194,21 @@
     slots = jnp.sum(order_hot * resume_slot[None, :], axis=1)
     ends = jnp.cumsum(lengths)
     starts = ends - lengths
+    every_id = jnp.arange(blocks * devices, dtype=jnp.int32)
+    inside = (
+        (every_id[:, None] >= starts[None, :]) & (every_id[:, None] < ends[None, :])
+    ).astype(jnp.int32)
+    every_slot = jnp.sum(inside * slots[None, :], axis=1)
+    every_first = jnp.any(every_id[:, None] == starts[None, :], axis=1).astype(jnp.float32)
+    every_pick = (
+        every_slot[:, None] == jnp.arange(BANK, dtype=jnp.int32)[None, :]
+    ).astype(jnp.float32)
     stream_ids = jnp.arange(blocks, dtype=jnp.int32) * devices + place
-    inside = (
-        (stream_ids[:, None] >= starts[None, :]) & (stream_ids[:, None] < ends[None, :])
-    ).astype(jnp.int32)
-    block_slot = jnp.sum(inside * slots[None, :], axis=1)
     first = jnp.any(stream_ids[:, None] == starts[None, :], axis=1)
+    block_slot = jnp.sum(
+        jnp.where(stream_ids[:, None] == every_id[None, :], every_slot[None, :], 0), axis=1
+    )
     pick = (block_slot[:, None] == jnp.arange(BANK, dtype=jnp.int32)[None, :]).astype(jnp.float32)
-    bank_state = jnp.einsum("cr,rhpn->chpn", pick, state_bank, precision=lax.Precision.HIGHEST)
     bank_rows = jnp.concatenate(
         [conv_bank_x, conv_bank_bc.reshape(BANK, KERNEL - 1, 2 * gstate_dev)], axis=2
     )
@@ -133,26 +243,20 @@
     local_state = jnp.einsum(
         "cqgjp,cqgn->cgjpn", weighted, bs, preferred_element_type=jnp.float32
     ).reshape(blocks, heads_dev, HEAD_DIM, STATE)
-    step_a = jnp.where(first[:, None], 0.0, grow)
-    step_b = local_state + jnp.where(
-        first[:, None, None, None], grow[:, :, None, None] * bank_state, 0.0
-    )
-    carry = jnp.zeros((heads_dev, HEAD_DIM, STATE), jnp.float32)
-    found = []
-    for row in range(blocks):
-        own = (step_a[row], step_b[row])
-        unit = (jnp.ones_like(own[0]), jnp.zeros_like(own[1]))
-        prior_a, prior_b = entering(own, "seq", combine, unit)
-        found.append(prior_a[:, None, None] * carry + prior_b)
-        whole_a, whole_b = combine((prior_a, prior_b), own)
-        carry = broadcast(whole_a[:, None, None] * carry + whole_b, "seq", devices - 1)
-    previous = jnp.stack(found, axis=0)
-    state_in = jnp.where(first[:, None, None, None], bank_state, previous)
+    state_in = entering_states(
+        local_state.reshape(blocks, heads_dev * HEAD_DIM, STATE),
+        grow,
+        every_pick,
+        every_first,
+        state_bank.reshape(BANK, heads_dev * HEAD_DIM, STATE),
+        place,
+        devices,
+    )
     read = jnp.einsum(
         "cqgn,cgjpn->cqgjp",
-        cq.astype(jnp.float32),
+        cq,
         state_in.reshape(blocks, groups_dev, per_group, HEAD_DIM, STATE),
-        precision=lax.Precision.HIGHEST,
+        preferred_element_type=jnp.float32,
     )
     growth = jnp.exp(cum).reshape(blocks, BLOCK, groups_dev, per_group, 1)
     skip = d_skip.reshape(1, 1, groups_dev, per_group, 1)

time: 326 us -> 128 us (0.39)
  waiting for transfers between devices: 180 us -> 11.7 us
  blocking collectives: 35 us -> 0 us
  Pallas kernels: 0 us -> 26.9 us
  other arithmetic: 31.2 us -> 10.7 us
  between operations: 13.7 us -> 0.55 us
  local copies, waits for them, and re-layouts: 33.7 us -> 44.3 us
  starting transfers between devices: 1.82 us -> 6.05 us
    all_gather x3 -> x0, waiting for transfers between devices: 113 us -> none  [the longest x2 95.1 us: entering(): pieces = jax.tree.map(lambda part: lax.all_gather(part, axis), value)]
    psum x1 -> x0, waiting for transfers between devices: 65.3 us -> none  [broadcast(): return lax.psum(block, axis)]
    all_gather x2 -> x0, blocking collectives: 35 us -> none  [entering(): pieces = jax.tree.map(lambda part: lax.all_gather(part, axis), value)]
    pallas_call x0 -> x1, Pallas kernels: none -> 26.9 us  [entering_states(): pl.pallas_call(functools.partial(exchange_kernel, count, blocks), out_sha...]
    select_n x29 -> x0, other arithmetic: 18 us -> none  [the longest x28 16.8 us: turn(): jnp.where(position < mine, new, old)]
    dynamic_update_slice x0 -> x7, local copies, waits for them, and re-layouts: none -> 7.91 us  [gather_columns(): lax.dynamic_update_slice_in_dim(whole, part, (mine ^ bits) * width, axis=1)]
    ppermute x0 -> x6, waiting for transfers between devices: none -> 7.31 us  [swap(): lax.ppermute(value, axis, [(source, source ^ bit) for source in range(cou...]
    ppermute x0 -> x6, starting transfers between devices: none -> 4.09 us  [swap(): lax.ppermute(value, axis, [(source, source ^ bit) for source in range(cou...]
  transfers between devices with their start and end apart: 5 -> 7, of which waited for: 5 -> 2; matrix products, arithmetic and copies ran while one was open for 15% -> 24% of each run, Pallas kernels for 0% -> 0%
where the time goes in v1:
time: 128 us; the launch traced here: 127 us
  local copies, waits for them, and re-layouts  44.3 us (35%)
  Pallas kernels  26.9 us (21%)
  matrix products  26.7 us (21%)
  waiting for transfers between devices  11.7 us (9%)
  other arithmetic  10.7 us (8%)
  starting transfers between devices  6.05 us (5%)
    pallas_call x1, Pallas kernels, entering_states(): pl.pallas_call(functools.partial(exchange_kernel, count, blocks), out_sha...  26.9 us
    unnamed x64, local copies, waits for them, and re-layouts  18.5 us
    dot_general x2, matrix products, per_device(): jnp.dot(piece, flat_zx, preferred_element_type=jnp.float32)  12.9 us
    dynamic_update_slice x7, local copies, waits for them, and re-layouts, gather_columns(): lax.dynamic_update_slice_in_dim(whole, part, (mine ^ bits) * width, axis=1)  7.91 us
    ppermute x6, waiting for transfers between devices, swap(): lax.ppermute(value, axis, [(source, source ^ bit) for source in range(cou...  7.31 us
    reshape x2, local copies, waits for them, and re-layouts, per_device(): y_total.reshape(rows_dev, inner_dev) * jax.nn.silu(gate.astype(jnp.float32))  7.25 us
    ppermute x1, waiting for transfers between devices, from_behind(): return lax.ppermute(value, axis, pairs)  4.38 us
    ppermute x6, starting transfers between devices, swap(): lax.ppermute(value, axis, [(source, source ^ bit) for source in range(cou...  4.09 us
  transfers between devices with their start and end apart: 7, of which 2 were waited for; matrix products, arithmetic and copies ran while one was open for 24% of the time, Pallas kernels for 0%

profile of v1, /device:TPU:0, one launch (start us, length us, event | category | flops | bytes accessed | tf_op | source)
XLA Modules:
  0.0 126.9 jit_solution(3334077629160959704)
XLA Ops:
  0.3 1.0 copy-done.4
  1.3 1.1 fusion.50
  3.0 2.6 %collective-permute-start.1 = (bf16[256,1024]{1,0:T(8,128)(2,1)}, bf16[256,1024]{1,0:T(8,128)(2,1)}, u32[]{:S(2)}, u32[]{:S(2)}) collective-permute-start(bf16[256,1024]{1,0:T(8,128)(2,1)} %get-tuple-element.17), channel_id=1, source_target_pairs={{0,2},{1,3},{2,0},{3,1},{4,6},{5,7},{6,4},{7,5},{8,10},{9,11},{10,... | collective-permute-start | bytes 1572872 | tf_op jit(solution)/shard_map/ppermute | solution.py:129
  7.3 1.6 %broadcast.123.clone = bf16[256,4096]{1,0:T(8,128)(2,1)} broadcast(bf16[]{:T(256)} %constant.23.clone.1), dimensions={} | broadcast | bytes 2097154 | tf_op jit(solution)/shard_map/broadcast.9
  11.4 7.3 %collective-permute-done.1 = bf16[256,1024]{1,0:T(8,128)(2,1)} collective-permute-done((bf16[256,1024]{1,0:T(8,128)(2,1)}, bf16[256,1024]{1,0:T(8,128)(2,1)}, u32[]{:S(2)}, u32[]{:S(2)}) %collective-permute-start.1) | collective-permute-done | bytes 524320 | tf_op jit(solution)/shard_map/ppermute | solution.py:129
  19.4 17.1 %copy.106 = bf16[512,8,2,1024]{3,1,2,0:T(8,128)(2,1)} copy(bf16[512,8,2,1024]{3,2,1,0:T(2,128)(2,1)} %bitcast.119) | data formatting | bytes 33554432
  37.1 1.1 constant_dynamic-update-slice_fusion.8
  38.2 1.1 constant_dynamic-update-slice_fusion.7
  39.3 2.0 %constant_dynamic-update-slice_fusion.4 = bf16[256,4096]{1,0:T(8,128)(2,1)} fusion(bf16[256,4096]{1,0:T(8,128)(2,1)} %constant_dynamic-update-slice_fusion.5, bf16[256,1024]{1,0:T(8,128)(2,1)} %collective-permute-done.3, s32[]{:T(128)S(6)} %select_n.48), kind=kLoop, calls=%fused_computation.83 | loop fusion | bytes 1048580 | tf_op jit(solution)/shard_map/dynamic_update_slice | solution.py:139
  41.4 1.9 %constant_dynamic-update-slice_fusion.3 = bf16[256,4096]{1,0:T(8,128)(2,1)} fusion(bf16[256,4096]{1,0:T(8,128)(2,1)} %constant_dynamic-update-slice_fusion.4, bf16[256,1024]{1,0:T(8,128)(2,1)} %collective-permute-done.4, s32[]{:T(128)S(6)} %select_n.49), kind=kLoop, calls=%fused_computation.82 | loop fusion | bytes 1048580 | tf_op jit(solution)/shard_map/dynamic_update_slice | solution.py:139
  44.8 0.9 constant_dynamic-update-slice_fusion.2
  45.6 3.0 %fusion.52 = f32[256,16]{0,1:T(8,128)S(1)} fusion(bf16[256,4096]{1,0:T(8,128)(2,1)} %constant_dynamic-update-slice_fusion.2, bf16[4096,16]{0,1:T(8,128)(2,1)S(1)} %copy-done.9), kind=kOutput, calls=%fused_computation.119 | convolution fusion | flops 33554432 | bytes 2244608 | tf_op jit(solution)/shard_map/dot_general | solution.py:183
  48.6 2.6 %fusion.26 = bf16[256,256]{1,0:T(8,128)(2,1)S(1)} fusion(bf16[256,4096]{1,0:T(8,128)(2,1)} %constant_dynamic-update-slice_fusion.2, bf16[512,8,2,128]{3,2,1,0:T(2,128)(2,1)S(1)} %bitcast.139), kind=kOutput, calls=%fused_computation.44 | convolution fusion | flops 536936448 | bytes 4325376 | tf_op jit(solution)/shard_map/dot_general | solution.py:182
  51.2 7.3 %convolution_convert_fusion = bf16[256,2048]{1,0:T(8,128)(2,1)} fusion(bf16[256,4096]{1,0:T(8,128)(2,1)} %constant_dynamic-update-slice_fusion.2, bf16[4096,2048]{1,0:T(8,128)(2,1)S(1)} %bitcast.120), kind=kOutput, calls=%fused_computation.19 | convolution fusion | flops 4295491584 | bytes 19922944 | tf_op jit(solution)/shard_map/dot_general | solution.py:181
  58.5 5.7 %convolution_convert_fusion.1 = bf16[256,2048]{1,0:T(8,128)(2,1)} fusion(bf16[256,4096]{1,0:T(8,128)(2,1)S(1)} %constant_dynamic-update-slice_fusion.6, bf16[4096,2048]{1,0:T(8,128)(2,1)S(1)} %bitcast.121), kind=kOutput, calls=%fused_computation.20 | convolution fusion | flops 4295491584 | bytes 19922944 | tf_op jit(solution)/shard_map/dot_general | solution.py:181
  64.2 1.2 reduce-window.18
  65.9 1.3 %fusion.29 = bf16[512,1024]{1,0:T(8,128)(2,1)S(1)} fusion(bf16[256,2048]{1,0:T(8,128)(2,1)} %convolution_convert_fusion.1, bf16[256,2048]{1,0:T(8,128)(2,1)} %convolution_convert_fusion), kind=kLoop, calls=%fused_computation.45 | loop fusion | flops 2097152 | bytes 3145728 | tf_op jit(solution)/shard_map/concatenate | solution.py:184
  67.3 2.0 %collective-permute-start.6 = (bf16[2,3,1280]{2,0,1:T(2,128)(2,1)S(1)}, bf16[2,3,1280]{2,0,1:T(2,128)(2,1)S(1)}, u32[]{:S(2)}, u32[]{:S(2)}) collective-permute-start(bf16[2,3,1280]{2,0,1:T(2,128)(2,1)S(1)} %copy.100), channel_id=1, source_target_pairs={{0,4},{4,8},{8,12},{12,16},{16,20},{20,24},{24,28},{28,0},{1,5},{5... | collective-permute-start | bytes 46088 | tf_op jit(solution)/shard_map/ppermute | solution.py:21
  69.7 4.4 %collective-permute-done.6 = bf16[2,3,1280]{2,0,1:T(2,128)(2,1)S(1)} collective-permute-done((bf16[2,3,1280]{2,0,1:T(2,128)(2,1)S(1)}, bf16[2,3,1280]{2,0,1:T(2,128)(2,1)S(1)}, u32[]{:S(2)}, u32[]{:S(2)}) %collective-permute-start.6) | collective-permute-done | bytes 15392 | tf_op jit(solution)/shard_map/ppermute | solution.py:21
  74.6 1.9 %multiply_convert_fusion.2 = bf16[2,256,1280]{2,1,0:T(8,128)(2,1)S(1)} fusion(f32[2,259,1280]{2,1,0:T(8,128)S(1)} %maximum_convert_fusion, f32[1280]{0:T(1024)S(1)} %get-tuple-element.8, f32[1280]{0:T(1024)S(1)} %get-tuple-element.9, f32[1280]{0:T(1024)S(1)} %get-tuple-element.10, f32[1280]{0:T(1024)S(1)} %get-tuple-element.7, f32[1280]{0:T(1024)S(1)} %pad_maximum_fusion.4), kind=kLoop, calls=%fused_computation.18 | loop fusion | flops 8519680 | bytes 11822080 | tf_op jit(solution)/shard_map/convert_element_type | solution.py:223
  76.5 1.2 fusion.35
  78.1 1.9 %copy.93 = f32[2,256,1024]{1,2,0:T(8,128)} copy(f32[2,256,1024]{2,1,0:T(8,128)S(1)} %get-tuple-element.15) | data formatting | bytes 4194304 | tf_op jit(solution)/shard_map/convert_element_type | solution.py:242
  80.5 1.5 %convolution_convert_fusion.3 = bf16[2,16,64,128]{3,2,1,0:T(8,128)(2,1)S(1)} fusion(bf16[2,256,16,64]{1,3,2,0:T(8,128)(2,1)S(1)} %bitcast.127, f32[2,256,16]{1,2,0:T(8,128)S(1)} %get-tuple-element.21, bf16[2,256,1280]{2,1,0:T(8,128)(2,1)} %copy-done.3), kind=kOutput, calls=%fused_computation.42 | convolution fusion | flops 136052736 | bytes 1736704 | tf_op jit(solution)/shard_map/cqgjp,cqgn->cgjpn/dot_general | solution.py:243
  82.0 0.9 copy_bitcast_fusion.local_ref
  84.2 26.9 %exchange.1 = bf16[8,2,128,128]{3,2,1,0:T(8,128)(2,1)} custom-call(bf16[8,2,128,128]{3,2,1,0:T(8,128)(2,1)} %copy_bitcast_fusion.local_ref, f32[8,8,128]{2,1,0:T(8,128)} %broadcast_in_dim.37.grow_ref, f32[16,8,128]{2,1,0:T(8,128)} %broadcast_in_dim.38.pick_ref, f32[2,128,128]{2,1,0:T(8,128)} %constant_dynamic-slice_fusion.bank_ref), custom_call_target="tpu_custom_call" | custom-call | tf_op jit(solution)/shard_map/exchange/pallas_call | solution.py:110
  111.2 1.2 copy.92
  112.4 1.3 %fusion.31 = f32[2,16,64,256]{3,2,1,0:T(8,128)S(1)} fusion(bf16[2,16,64,128]{3,2,1,0:T(8,128)(2,1)S(1)} %bitcast.126, bf16[2,256,1280]{2,1,0:T(8,128)(2,1)} %copy-done.3), kind=kOutput, calls=%fused_computation.50 | convolution fusion | flops 134217728 | bytes 2752512 | tf_op jit(solution)/shard_map/cqgn,cgjpn->cqgjp/dot_general | solution.py:255
  113.8 2.6 %fusion.20 = f32[2,256,1,16,64]{1,4,3,0,2:T(8,128)S(1)} fusion(f32[2,16,64,256]{3,2,1,0:T(8,128)S(1)} %fusion.31, f32[2,256,1,16,64]{1,4,3,0,2:T(8,128)S(1)} %bitcast.124, bf16[2,256,16,64]{1,3,2,0:T(8,128)(2,1)S(1)} %bitcast.128, f32[2,16,256]{2,1,0:T(8,128)S(1)} %get-tuple-element.20, f32[2,16,256]{2,1,0:T(8,128)S(1)} %get-tuple-element.23, ...), kind=kOutput, calls=%fused_computation.34 | convolution fusion | flops 281018368 | bytes 8028224 | tf_op jit(solution)/shard_map/cgjqk,ckgjp->cqgjp/dot_general | solution.py:238
  116.4 3.8 %copy.98 = f32[2,256,1,16,64]{4,3,1,0,2:T(8,128)} copy(f32[2,256,1,16,64]{1,4,3,0,2:T(8,128)S(1)} %fusion.20) | data formatting | bytes 4194304 | tf_op jit(solution)/shard_map/reshape | solution.py:264
  120.2 3.5 %reshape.253 = f32[512,1024]{1,0:T(8,128)S(1)} reshape(f32[2,256,1,16,64]{4,3,1,0,2:T(8,128)} %copy.98) | data formatting | bytes 4194304 | tf_op jit(solution)/shard_map/reshape | solution.py:264
  123.7 2.0 %multiply_reduce_fusion = (f32[512]{0:T(512)S(1)}, f32[512,1024]{1,0:T(8,128)S(1)}) fusion(f32[512,1024]{1,0:T(8,128)S(1)} %reshape.253, bf16[256,2048]{1,0:T(8,128)(2,1)} %convolution_convert_fusion, bf16[256,2048]{1,0:T(8,128)(2,1)} %convolution_convert_fusion.1), kind=kLoop, calls=%fused_computation.36 | loop fusion | flops 5766656 | bytes 6293504 | tf_op jit(solution)/shard_map/reduce_sum | solution.py:266
  125.7 1.2 multiply_convert_fusion.3
  (118 shorter events, 11.4 us)
Async XLA Ops:
  0.0 9.8 %copy-start = (f32[2,16,64,128]{3,2,1,0:T(8,128)S(1)}, f32[2,16,64,128]{3,2,1,0:T(8,128)}, u32[]{:S(2)}) copy-start(f32[2,16,64,128]{3,2,1,0:T(8,128)} %param.30) | copy-start | bytes 3145732
  0.0 6.0 %copy-start.20 = (s32[3]{0:T(128)S(1)}, s32[3]{0:T(128)}, u32[]{:S(2)}) copy-start(s32[3]{0:T(128)} %param.35) | copy-start | bytes 40
  0.0 6.0 %copy-start.21 = (s32[3]{0:T(128)S(1)}, s32[3]{0:T(128)}, u32[]{:S(2)}) copy-start(s32[3]{0:T(128)} %param.34) | copy-start | bytes 40
  0.0 6.0 %copy-start.22 = (s32[3]{0:T(128)S(1)}, s32[3]{0:T(128)}, u32[]{:S(2)}) copy-start(s32[3]{0:T(128)} %param.33) | copy-start | bytes 40
  0.0 7.3 %copy-start.11 = (f32[4,1024]{1,0:T(4,128)S(1)}, f32[4,1024]{1,0:T(4,128)}, u32[]{:S(2)}) copy-start(f32[4,1024]{1,0:T(4,128)} %param.22) | copy-start | bytes 49156
  2.4 7.4 %copy-start.13 = (f32[4,2,128]{2,1,0:T(2,128)S(1)}, f32[4,2,128]{2,1,0:T(2,128)}, u32[]{:S(2)}) copy-start(f32[4,2,128]{2,1,0:T(2,128)} %param.24) | copy-start | bytes 12292
  2.4 8.8 %copy-start.25 = (f32[16]{0:T(128)S(1)}, f32[16]{0:T(128)}, u32[]{:S(2)}) copy-start(f32[16]{0:T(128)} %param.26) | copy-start | bytes 196
  2.4 8.8 %copy-start.14 = (f32[1024]{0:T(1024)S(1)}, f32[1024]{0:T(1024)}, u32[]{:S(2)}) copy-start(f32[1024]{0:T(1024)} %param.23) | copy-start | bytes 12292
  2.5 8.8 %copy-start.19 = (f32[2,128]{1,0:T(2,128)S(1)}, f32[2,128]{1,0:T(2,128)}, u32[]{:S(2)}) copy-start(f32[2,128]{1,0:T(2,128)} %param.25) | copy-start | bytes 3076
  2.5 16.3 %copy-start.15 = (bf16[2,3,2,128]{3,2,1,0:T(2,128)(2,1)S(1)}, bf16[2,3,2,128]{3,2,1,0:T(2,128)(2,1)}, u32[]{:S(2)}) copy-start(bf16[2,3,2,128]{3,2,1,0:T(2,128)(2,1)} %param.32) | copy-start | bytes 9220
  2.5 34.6 %collective-permute-start = (bf16[256,1024]{1,0:T(8,128)(2,1)}, bf16[256,1024]{1,0:T(8,128)(2,1)}, u32[]{:S(2)}, u32[]{:S(2)}) collective-permute-start(bf16[256,1024]{1,0:T(8,128)(2,1)} %get-tuple-element.17), channel_id=1, source_target_pairs={{0,1},{1,0},{2,3},{3,2},{4,5},{5,4},{6,7},{7,6},{8,9},{9,8},{10,11... | collective-permute-start | bytes 1572872 | tf_op jit(solution)/shard_map/ppermute | solution.py:129
  3.0 15.7 %collective-permute-start.1 = (bf16[256,1024]{1,0:T(8,128)(2,1)}, bf16[256,1024]{1,0:T(8,128)(2,1)}, u32[]{:S(2)}, u32[]{:S(2)}) collective-permute-start(bf16[256,1024]{1,0:T(8,128)(2,1)} %get-tuple-element.17), channel_id=1, source_target_pairs={{0,2},{1,3},{2,0},{3,1},{4,6},{5,7},{6,4},{7,5},{8,10},{9,11},{10,... | collective-permute-start | bytes 1572872 | tf_op jit(solution)/shard_map/ppermute | solution.py:129
  5.6 33.7 %collective-permute-start.3 = (bf16[256,1024]{1,0:T(8,128)(2,1)}, bf16[256,1024]{1,0:T(8,128)(2,1)}, u32[]{:S(2)}, u32[]{:S(2)}) collective-permute-start(bf16[256,1024]{1,0:T(8,128)(2,1)} %get-tuple-element.19), channel_id=1, source_target_pairs={{0,1},{1,0},{2,3},{3,2},{4,5},{5,4},{6,7},{7,6},{8,9},{9,8},{10,11... | collective-permute-start | bytes 1572872 | tf_op jit(solution)/shard_map/ppermute | solution.py:129
  5.7 30.8 %collective-permute-start.4 = (bf16[256,1024]{1,0:T(8,128)(2,1)}, bf16[256,1024]{1,0:T(8,128)(2,1)}, u32[]{:S(2)}, u32[]{:S(2)}) collective-permute-start(bf16[256,1024]{1,0:T(8,128)(2,1)} %get-tuple-element.19), channel_id=1, source_target_pairs={{0,2},{1,3},{2,0},{3,1},{4,6},{5,7},{6,4},{7,5},{8,10},{9,11},{10,... | collective-permute-start | bytes 1572872 | tf_op jit(solution)/shard_map/ppermute | solution.py:129
  6.4 2.5 %copy-start.5 = (bf16[512,1024]{1,0:T(8,128)(2,1)S(1)}, bf16[512,1024]{1,0:T(8,128)(2,1)}, u32[]{:S(2)}) copy-start(bf16[512,1024]{1,0:T(8,128)(2,1)} %param.18) | copy-start | bytes 3145732
  18.7 24.6 %collective-permute-start.2 = (bf16[256,1024]{1,0:T(8,128)(2,1)}, bf16[256,1024]{1,0:T(8,128)(2,1)S(1)}, u32[]{:S(2)}, u32[]{:S(2)}) collective-permute-start(bf16[256,1024]{1,0:T(8,128)(2,1)} %collective-permute-done.1), channel_id=1, source_target_pairs={{0,1},{1,0},{2,3},{3,2},{4,5},{5,4},{6,7},{7,6},{8,9},{9,8},{10,11... | collective-permute-start | bytes 1572872 | tf_op jit(solution)/shard_map/ppermute | solution.py:129
  36.5 8.2 %collective-permute-start.5 = (bf16[256,1024]{1,0:T(8,128)(2,1)}, bf16[256,1024]{1,0:T(8,128)(2,1)S(1)}, u32[]{:S(2)}, u32[]{:S(2)}) collective-permute-start(bf16[256,1024]{1,0:T(8,128)(2,1)} %collective-permute-done.4), channel_id=1, source_target_pairs={{0,1},{1,0},{2,3},{3,2},{4,5},{5,4},{6,7},{7,6},{8,9},{9,8},{10,11... | collective-permute-start | bytes 1572872 | tf_op jit(solution)/shard_map/ppermute | solution.py:129
  38.2 5.2 %copy-start.9 = (bf16[4096,16]{0,1:T(8,128)(2,1)S(1)}, bf16[4096,16]{0,1:T(8,128)(2,1)}, u32[]{:S(2)}) copy-start(bf16[4096,16]{0,1:T(8,128)(2,1)} %param.21) | copy-start | bytes 393220
  39.3 4.7 %copy-start.23 = (bf16[4096,2,128]{2,1,0:T(2,128)(2,1)S(1)}, bf16[4096,2,128]{2,1,0:T(2,128)(2,1)}, u32[]{:S(2)}) copy-start(bf16[4096,2,128]{2,1,0:T(2,128)(2,1)} %param.20) | copy-start | bytes 6291460
  43.3 7.9 %copy-start.2 = (bf16[512,8,2,1024]{3,1,2,0:T(8,128)(2,1)S(1)}, bf16[512,8,2,1024]{3,1,2,0:T(8,128)(2,1)}, u32[]{:S(2)}) copy-start(bf16[512,8,2,1024]{3,1,2,0:T(8,128)(2,1)} %copy.106) | copy-start | bytes 50331652
  58.5 5.7 %copy-start.17 = (f32[16]{0:T(128)S(1)}, f32[16]{0:T(128)}, u32[]{:S(2)}) copy-start(f32[16]{0:T(128)} %param.27) | copy-start | bytes 196
  67.2 6.9 %copy-start.16 = (bf16[2,3,256]{2,0,1:T(2,128)(2,1)S(1)}, bf16[2,3,256]{2,0,1:T(2,128)(2,1)}, u32[]{:S(2)}) copy-start(bf16[2,3,256]{2,0,1:T(2,128)(2,1)} %reshape.236) | copy-start | bytes 9220
  67.2 6.9 %copy-start.24 = (bf16[2,3,1024]{2,0,1:T(2,128)(2,1)S(1)}, bf16[2,3,1024]{2,0,1:T(2,128)(2,1)}, u32[]{:S(2)}) copy-start(bf16[2,3,1024]{2,0,1:T(2,128)(2,1)} %param.31) | copy-start | bytes 36868
  67.2 6.9 %copy-start.27 = (pred[2]{0:T(512)(128)(4,1)S(1)}, pred[2]{0:T(512)(128)(4,1)}, u32[]{:S(2)}) copy-start(pred[2]{0:T(512)(128)(4,1)} %compare_reduce_fusion) | copy-start | bytes 10
  67.2 6.9 %copy-start.28 = (s32[2]{0:T(128)S(1)}, s32[2]{0:T(128)}, u32[]{:S(2)}) copy-start(s32[2]{0:T(128)} %fusion.42) | copy-start | bytes 28
  67.3 6.7 %collective-permute-start.6 = (bf16[2,3,1280]{2,0,1:T(2,128)(2,1)S(1)}, bf16[2,3,1280]{2,0,1:T(2,128)(2,1)S(1)}, u32[]{:S(2)}, u32[]{:S(2)}) collective-permute-start(bf16[2,3,1280]{2,0,1:T(2,128)(2,1)S(1)} %copy.100), channel_id=1, source_target_pairs={{0,4},{4,8},{8,12},{12,16},{16,20},{20,24},{24,28},{28,0},{1,5},{5... | collective-permute-start | bytes 46088 | tf_op jit(solution)/shard_map/ppermute | solution.py:21
  80.5 30.7 %copy-start.7 = (bf16[2,256,1024]{1,2,0:T(8,128)(2,1)}, bf16[2,256,1024]{1,2,0:T(8,128)(2,1)S(1)}, u32[]{:S(2)}) copy-start(bf16[2,256,1024]{1,2,0:T(8,128)(2,1)S(1)} %copy.84) | copy-start | bytes 3145732
  111.2 2.6 %copy-start.6 = (f32[2,256,1024]{1,2,0:T(8,128)S(1)}, f32[2,256,1024]{1,2,0:T(8,128)}, u32[]{:S(2)}) copy-start(f32[2,256,1024]{1,2,0:T(8,128)} %copy.93) | copy-start | bytes 6291460
  111.2 2.6 %copy-start.10 = (f32[2,256,256]{2,1,0:T(8,128)S(1)}, f32[2,256,256]{2,1,0:T(8,128)}, u32[]{:S(2)}) copy-start(f32[2,256,256]{2,1,0:T(8,128)} %fusion.35) | copy-start | bytes 1572868
  111.2 2.6 %copy-start.26 = (f32[16]{0:T(128)S(1)}, f32[16]{0:T(128)}, u32[]{:S(2)}) copy-start(f32[16]{0:T(128)} %param.28) | copy-start | bytes 196
  111.2 2.6 %copy-start.8 = (bf16[2,256,1024]{1,2,0:T(8,128)(2,1)S(1)}, bf16[2,256,1024]{1,2,0:T(8,128)(2,1)}, u32[]{:S(2)}) copy-start(bf16[2,256,1024]{1,2,0:T(8,128)(2,1)} %copy-done.7) | copy-start | bytes 3145732
  123.7 3.2 %copy-start.1 = (f32[2,16,64,128]{3,2,1,0:T(8,128)S(1)}, f32[2,16,64,128]{3,2,1,0:T(8,128)}, u32[]{:S(2)}) copy-start(f32[2,16,64,128]{3,2,1,0:T(8,128)} %param.30) | copy-start | bytes 3145732
  (4 other events, 7.1 us)

commit v2 on v1

--- a/solution.py
+++ b/solution.py
@@ -129,15 +129,81 @@
     return lax.ppermute(value, axis, [(source, source ^ bit) for source in range(count)])
 
 
-def gather_columns(rows, axis):
-    mine, width = lax.axis_index(axis), rows.shape[1]
-    far = swap(rows, axis, 2)
-    near = swap(rows, axis, 1)
-    both = swap(far, axis, 1)
-    whole = jnp.zeros((rows.shape[0], width * 4), rows.dtype)
-    for bits, part in ((0, rows), (1, near), (2, far), (3, both)):
-        whole = lax.dynamic_update_slice_in_dim(whole, part, (mine ^ bits) * width, axis=1)
-    return whole
+def gather_columns(hidden, axis, weights):
+    mine, (rows, width) = lax.axis_index(axis), hidden.shape
+    starts = range(0, rows, BLOCK)
+    own = [hidden[start : start + BLOCK] for start in starts]
+    far = [swap(part, axis, 2) for part in own]
+    near = [swap(part, axis, 1) for part in own]
+    far, weights = lax.optimization_barrier((far, weights))
+    both = [swap(part, axis, 1) for part in far]
+    wholes = []
+    for parts in zip(own, near, far, both):
+        whole = jnp.zeros((BLOCK, width * 4), hidden.dtype)
+        for bits, part in enumerate(parts):
+            whole = lax.dynamic_update_slice_in_dim(whole, part, (mine ^ bits) * width, axis=1)
+        wholes.append(whole)
+    return wholes, weights
+
+
+def tail_kernel(
+    per_group, cum_ref, cum_t_ref, dt_t_ref, xs_ref, bs_ref, cs_ref, gate_ref, state_ref,
+    skip_ref, gain_ref, out_ref, y_ref,
+):
+    tokens, heads = cum_ref.shape[1:]
+    lower = lax.broadcasted_iota(jnp.int32, (tokens, tokens), 0) >= lax.broadcasted_iota(
+        jnp.int32, (tokens, tokens), 1
+    )
+    across = (((1,), (1,)), ((), ()))
+    wide = per_group * HEAD_DIM
+    for group in range(heads // per_group):
+        of_group = slice(group * STATE, (group + 1) * STATE)
+        channels = slice(group * wide, (group + 1) * wide)
+        cs = cs_ref[0, :, of_group]
+        scores = lax.dot_general(
+            cs, bs_ref[0, :, of_group], across, preferred_element_type=jnp.float32
+        )
+        y_ref[:, channels] = lax.dot_general(
+            cs, state_ref[0, channels, :], across, preferred_element_type=jnp.float32
+        )
+        for head in range(group * per_group, (group + 1) * per_group):
+            here = slice(head * HEAD_DIM, (head + 1) * HEAD_DIM)
+            cum = cum_ref[0, :, head : head + 1]
+            diff = cum - cum_t_ref[0, head : head + 1, :]
+            damp = jnp.exp(jnp.where(lower, diff, -jnp.inf))
+            mix = (scores * damp * dt_t_ref[0, head : head + 1, :]).astype(jnp.bfloat16)
+            y_ref[:, here] = jnp.exp(cum) * y_ref[:, here] + jnp.dot(
+                mix, xs_ref[0, :, here], preferred_element_type=jnp.float32
+            )
+        gate = gate_ref[0, :, channels].astype(jnp.float32)
+        y = y_ref[:, channels] + skip_ref[:, channels] * xs_ref[0, :, channels].astype(jnp.float32)
+        gated = y * (gate / (1.0 + jnp.exp(-gate)))
+        mean = jnp.mean(gated * gated, axis=1, keepdims=True)
+        normed = gated * lax.rsqrt(mean + 1e-05) * gain_ref[:, channels]
+        out_ref[0, :, channels] = normed.astype(jnp.bfloat16)
+
+
+def finish(cum, dt, xs, bs, cs, gate, state_in, skip, gain, per_group):
+    blocks, _, inner = xs.shape
+
+    def each(array):
+        return pl.BlockSpec((1,) + array.shape[1:], lambda c: (c, 0, 0))
+
+    def fixed(array):
+        return pl.BlockSpec(array.shape, lambda c: (0, 0))
+
+    split = (cum, cum.transpose(0, 2, 1), dt.transpose(0, 2, 1), xs, bs, cs, gate, state_in)
+    shared = (skip, gain)
+    return pl.pallas_call(
+        functools.partial(tail_kernel, per_group),
+        grid=(blocks,),
+        out_shape=jax.ShapeDtypeStruct(xs.shape, jnp.bfloat16),
+        in_specs=[each(array) for array in split] + [fixed(array) for array in shared],
+        out_specs=each(xs),
+        scratch_shapes=[pltpu.VMEM((BLOCK, inner), jnp.float32)],
+        compiler_params=pltpu.CompilerParams(vmem_limit_bytes=32 * 1024 * 1024),
+        name="finish",
+    )(*split, *shared)
 
 
 def per_device(
@@ -173,15 +239,14 @@
     prompts = prompt_blocks.shape[0]
     flat_zx = w_zx.reshape(WIDTH, 2 * inner_dev)
     flat_bc = w_bc.reshape(WIDTH, 2 * gstate_dev)
-    pieces = []
-    for row in range(blocks):
-        pieces.append(gather_columns(hidden[row * BLOCK : (row + 1) * BLOCK], "mp"))
-    zx, bc, dt_raw = [], [], []
-    for piece in pieces:
-        zx.append(jnp.dot(piece, flat_zx, preferred_element_type=jnp.float32).astype(jnp.bfloat16))
-        bc.append(jnp.dot(piece, flat_bc, preferred_element_type=jnp.float32).astype(jnp.bfloat16))
-        dt_raw.append(jnp.dot(piece, w_dt, preferred_element_type=jnp.float32))
-    zx, bc, dt_raw = (jnp.concatenate(parts, axis=0) for parts in (zx, bc, dt_raw))
+    pieces, flat_zx = gather_columns(hidden, "mp", flat_zx)
+    zx = [
+        jnp.dot(piece, flat_zx, preferred_element_type=jnp.float32).astype(jnp.bfloat16)
+        for piece in pieces
+    ]
+    zx, piece = jnp.concatenate(zx, axis=0), jnp.concatenate(pieces, axis=0)
+    bc = jnp.dot(piece, flat_bc, preferred_element_type=jnp.float32).astype(jnp.bfloat16)
+    dt_raw = jnp.dot(piece, w_dt, preferred_element_type=jnp.float32)
     gate = zx[:, :inner_dev]
     mixin = jnp.concatenate([zx[:, inner_dev:], bc], axis=1).reshape(blocks, BLOCK, channels)
     own_tails = mixin[:, BLOCK - (KERNEL - 1) :, :]
@@ -223,19 +288,8 @@
     conv = jax.nn.silu(acc).astype(jnp.bfloat16)
     xs = conv[..., :inner_dev].reshape(blocks, BLOCK, groups_dev, per_group, HEAD_DIM)
     bs = conv[..., inner_dev : inner_dev + gstate_dev].reshape(blocks, BLOCK, groups_dev, STATE)
-    cq = conv[..., inner_dev + gstate_dev :].reshape(blocks, BLOCK, groups_dev, STATE)
     dt = jax.nn.softplus(dt_raw.reshape(blocks, BLOCK, heads_dev) + dt_bias[None, None, :])
     cum = jnp.cumsum(dt * (-jnp.exp(a_log))[None, None, :], axis=1)
-    scores = jnp.einsum("cqgn,ckgn->cgqk", cq, bs, preferred_element_type=jnp.float32)
-    cum_h = cum.transpose(0, 2, 1)
-    lower = jnp.arange(BLOCK)[:, None] >= jnp.arange(BLOCK)[None, :]
-    damp = jnp.exp(
-        jnp.where(lower[None, None], cum_h[:, :, :, None] - cum_h[:, :, None, :], -jnp.inf)
-    )
-    damp = damp.reshape(blocks, groups_dev, per_group, BLOCK, BLOCK)
-    dt_h = dt.transpose(0, 2, 1).reshape(blocks, groups_dev, per_group, 1, BLOCK)
-    mix = (scores[:, :, None] * damp * dt_h).astype(jnp.bfloat16)
-    y_intra = jnp.einsum("cgjqk,ckgjp->cqgjp", mix, xs, preferred_element_type=jnp.float32)
     last = cum[:, -1, :]
     grow = jnp.exp(last)
     factor = (dt * jnp.exp(last[:, None, :] - cum)).reshape(blocks, BLOCK, groups_dev, per_group, 1)
@@ -252,20 +306,19 @@
         place,
         devices,
     )
-    read = jnp.einsum(
-        "cqgn,cgjpn->cqgjp",
-        cq,
-        state_in.reshape(blocks, groups_dev, per_group, HEAD_DIM, STATE),
-        preferred_element_type=jnp.float32,
-    )
-    growth = jnp.exp(cum).reshape(blocks, BLOCK, groups_dev, per_group, 1)
-    skip = d_skip.reshape(1, 1, groups_dev, per_group, 1)
-    y_total = y_intra + growth * read + skip * xs.astype(jnp.float32)
-    gated = y_total.reshape(rows_dev, inner_dev) * jax.nn.silu(gate.astype(jnp.float32))
-    grouped = gated.reshape(rows_dev, groups_dev, inner_dev // groups_dev)
-    scale = lax.rsqrt(jnp.mean(grouped * grouped, axis=2, keepdims=True) + 1e-05)
-    result = (grouped * scale).reshape(rows_dev, inner_dev) * norm_gain[None, :]
-    return result.astype(jnp.bfloat16)
+    result = finish(
+        cum,
+        dt,
+        conv[..., :inner_dev],
+        conv[..., inner_dev : inner_dev + gstate_dev],
+        conv[..., inner_dev + gstate_dev :],
+        gate.reshape(blocks, BLOCK, inner_dev),
+        state_in,
+        jnp.repeat(d_skip, HEAD_DIM)[None, :],
+        norm_gain[None, :],
+        per_group,
+    )
+    return result.reshape(rows_dev, inner_dev)
 
 
 def solution(mesh):

time: 128 us -> 126 us (0.984)
  Pallas kernels: 26.9 us -> 34.4 us
  waiting for transfers between devices: 11.7 us -> 5.05 us
  local copies, waits for them, and re-layouts: 44.3 us -> 41.6 us
  matrix products: 26.7 us -> 28.6 us
  other arithmetic: 10.7 us -> 9.13 us
    pallas_call x0 -> x1, Pallas kernels: none -> 7.52 us  [finish(): pl.pallas_call(functools.partial(tail_kernel, per_group), grid=(blocks,),...]
    reshape x2 -> x0, local copies, waits for them, and re-layouts: 7.25 us -> none  [per_device(): y_total.reshape(rows_dev, inner_dev) * jax.nn.silu(gate.astype(jnp.float32))]
    dot_general x2, matrix products: 12.9 us -> 18.8 us  [per_device(): jnp.dot(piece, flat_zx, preferred_element_type=jnp.float32)]
    dot_general x5 -> x1, matrix products: 8.79 us -> 3.42 us  [per_device(): dt_raw = jnp.dot(piece, w_dt, preferred_element_type=jnp.float32)]
    ppermute x6, waiting for transfers between devices: 7.31 us -> 1.97 us  [swap(): lax.ppermute(value, axis, [(source, source ^ bit) for source in range(cou...]
    reduce_sum x2 -> x1, other arithmetic: 2.18 us -> 0.18 us  [per_device(): lengths = jnp.sum(order_hot * prompt_blocks[None, :], axis=1)]
    dynamic_update_slice x7 -> x8, local copies, waits for them, and re-layouts: 7.91 us -> 9.48 us  [gather_columns(): lax.dynamic_update_slice_in_dim(whole, part, (mine ^ bits) * width, axis=1)]
    another operation x3 -> x5, local copies, waits for them, and re-layouts: 1.82 us -> 3.33 us
  transfers between devices with their start and end apart: 7 -> 7, of which waited for: 2 -> 2; matrix products, arithmetic and copies ran while one was open for 24% -> 33% of each run, Pallas kernels for 0% -> 0%
where the time goes in v2:
time: 126 us; the launch traced here: 125 us
  local copies, waits for them, and re-layouts  41.6 us (33%)
  Pallas kernels  34.4 us (27%)
  matrix products  28.6 us (23%)
  other arithmetic  9.13 us (7%)
  starting transfers between devices  5.85 us (5%)
  waiting for transfers between devices  5.05 us (4%)
    pallas_call x1, Pallas kernels, entering_states(): pl.pallas_call(functools.partial(exchange_kernel, count, blocks), out_sha...  26.9 us
    unnamed x59, local copies, waits for them, and re-layouts  19.8 us
    dot_general x2, matrix products, per_device(): jnp.dot(piece, flat_zx, preferred_element_type=jnp.float32)  18.8 us
    dynamic_update_slice x8, local copies, waits for them, and re-layouts, gather_columns(): lax.dynamic_update_slice_in_dim(whole, part, (mine ^ bits) * width, axis=1)  9.48 us
    pallas_call x1, Pallas kernels, finish(): pl.pallas_call(functools.partial(tail_kernel, per_group), grid=(blocks,),...  7.52 us
    dot_general x1, matrix products, per_device(): jnp.dot(piece, flat_bc, preferred_element_type=jnp.float32)  4.19 us
    ppermute x6, starting transfers between devices, swap(): lax.ppermute(value, axis, [(source, source ^ bit) for source in range(cou...  4.07 us
    dot_general x1, matrix products, per_device(): dt_raw = jnp.dot(piece, w_dt, preferred_element_type=jnp.float32)  3.42 us
  transfers between devices with their start and end apart: 7, of which 2 were waited for; matrix products, arithmetic and copies ran while one was open for 33% of the time, Pallas kernels for 0%

profile of v2, /device:TPU:0, one launch (start us, length us, event | category | flops | bytes accessed | tf_op | source)
XLA Modules:
  0.0 125.0 jit_solution(5489794847182679322)
XLA Ops:
  0.0 1.6 %broadcast.67.clone.1 = bf16[256,4096]{1,0:T(8,128)(2,1)} broadcast(bf16[]{:T(256)} %constant.15.clone.1), dimensions={} | broadcast | bytes 2097154 | tf_op jit(solution)/shard_map/broadcast.7
  1.6 1.3 %constant_dynamic-update-slice_fusion.9 = (bf16[256,4096]{1,0:T(8,128)(2,1)}, bf16[256,1024]{1,0:T(8,128)(2,1)}, bf16[256,1024]{1,0:T(8,128)(2,1)}) fusion(bf16[256,4096]{1,0:T(8,128)(2,1)} %broadcast.67.clone.1, s32[]{:T(128)S(6)} %select_n.39, bf16[512,1024]{1,0:T(8,128)(2,1)S(1)} %copy-done.7), kind=kLoop, calls=%fused_computation.57 | loop fusion | bytes 2621444 | tf_op jit(solution)/shard_map/dynamic_update_slice | solution.py:144
  3.5 2.6 %collective-permute-start.2 = (bf16[256,1024]{1,0:T(8,128)(2,1)}, bf16[256,1024]{1,0:T(8,128)(2,1)}, u32[]{:S(2)}, u32[]{:S(2)}) collective-permute-start(bf16[256,1024]{1,0:T(8,128)(2,1)} %get-tuple-element.26), channel_id=1, source_target_pairs={{0,2},{1,3},{2,0},{3,1},{4,6},{5,7},{6,4},{7,5},{8,10},{9,11},{10,... | collective-permute-start | bytes 1572872 | tf_op jit(solution)/shard_map/ppermute | solution.py:129
  7.3 1.5 %broadcast.67.clone = bf16[256,4096]{1,0:T(8,128)(2,1)} broadcast(bf16[]{:T(256)} %constant.15.clone.1), dimensions={} | broadcast | bytes 2097154 | tf_op jit(solution)/shard_map/broadcast.7
  8.9 0.9 constant_dynamic-update-slice_fusion.5
  10.9 17.1 %copy.76 = bf16[512,8,2,1024]{3,1,2,0:T(8,128)(2,1)} copy(bf16[512,8,2,1024]{3,2,1,0:T(2,128)(2,1)} %bitcast.86) | data formatting | bytes 33554432
  28.1 2.0 %collective-permute-done.1 = bf16[256,1024]{1,0:T(8,128)(2,1)S(1)} collective-permute-done((bf16[256,1024]{1,0:T(8,128)(2,1)}, bf16[256,1024]{1,0:T(8,128)(2,1)S(1)}, u32[]{:S(2)}, u32[]{:S(2)}) %collective-permute-start.1) | collective-permute-done | bytes 524320 | tf_op jit(solution)/shard_map/ppermute | solution.py:129
  30.8 1.9 %constant_dynamic-update-slice_fusion.8 = bf16[256,4096]{1,0:T(8,128)(2,1)} fusion(bf16[256,4096]{1,0:T(8,128)(2,1)} %get-tuple-element.25, bf16[256,1024]{1,0:T(8,128)(2,1)} %collective-permute-done, s32[]{:T(128)S(6)} %select_n.40), kind=kLoop, calls=%fused_computation.56 | loop fusion | bytes 1048580 | tf_op jit(solution)/shard_map/dynamic_update_slice | solution.py:144
  32.7 0.9 constant_dynamic-update-slice_fusion.7
  33.6 0.9 constant_dynamic-update-slice_fusion.4
  34.5 1.9 %constant_dynamic-update-slice_fusion.3 = bf16[256,4096]{1,0:T(8,128)(2,1)} fusion(bf16[256,4096]{1,0:T(8,128)(2,1)} %constant_dynamic-update-slice_fusion.4, bf16[256,1024]{1,0:T(8,128)(2,1)} %collective-permute-done.2, s32[]{:T(128)S(6)} %select_n.41), kind=kLoop, calls=%fused_computation.51 | loop fusion | bytes 1048580 | tf_op jit(solution)/shard_map/dynamic_update_slice | solution.py:144
  36.4 0.9 constant_dynamic-update-slice_fusion.6
  37.3 11.5 %convolution_convert_fusion.1 = bf16[256,2048]{1,0:T(8,128)(2,1)S(1)} fusion(bf16[256,4096]{1,0:T(8,128)(2,1)} %constant_dynamic-update-slice_fusion.6, bf16[4096,2048]{1,0:T(8,128)(2,1)} %bitcast.87), kind=kOutput, calls=%fused_computation.13 | convolution fusion | flops 4295491584 | bytes 19922944 | tf_op jit(solution)/shard_map/dot_general | solution.py:244
  48.8 0.9 constant_dynamic-update-slice_fusion.2
  49.7 7.3 %convolution_convert_fusion = bf16[256,2048]{1,0:T(8,128)(2,1)} fusion(bf16[256,4096]{1,0:T(8,128)(2,1)} %constant_dynamic-update-slice_fusion.2, bf16[4096,2048]{1,0:T(8,128)(2,1)S(1)} %bitcast.90), kind=kOutput, calls=%fused_computation.12 | convolution fusion | flops 4295491584 | bytes 19922944 | tf_op jit(solution)/shard_map/dot_general | solution.py:244
  57.0 3.4 %fusion.1 = f32[512,16]{0,1:T(8,128)S(1)} fusion(bf16[4096,16]{0,1:T(8,128)(2,1)S(1)} %copy-done.20, bf16[256,4096]{1,0:T(8,128)(2,1)} %constant_dynamic-update-slice_fusion.2, bf16[256,4096]{1,0:T(8,128)(2,1)} %constant_dynamic-update-slice_fusion.6), kind=kOutput, calls=%fused_computation.2 | convolution fusion | flops 75497472 | bytes 4358144 | tf_op jit(solution)/shard_map/dot_general | solution.py:249
  60.5 1.2 reduce-window.14
  62.7 4.2 %fusion.8 = bf16[512,256]{1,0:T(8,128)(2,1)S(1)} fusion(bf16[512,8,2,128]{3,2,1,0:T(2,128)(2,1)} %bitcast.104, bf16[256,4096]{1,0:T(8,128)(2,1)} %constant_dynamic-update-slice_fusion.2, bf16[256,4096]{1,0:T(8,128)(2,1)} %constant_dynamic-update-slice_fusion.6), kind=kOutput, calls=%fused_computation.22 | convolution fusion | flops 1082261504 | bytes 6553600 | tf_op jit(solution)/shard_map/dot_general | solution.py:248
  67.3 1.8 %collective-permute-start.6 = (bf16[2,3,1280]{2,1,0:T(4,128)(2,1)S(1)}, bf16[2,3,1280]{2,1,0:T(4,128)(2,1)S(1)}, u32[]{:S(2)}, u32[]{:S(2)}) collective-permute-start(bf16[2,3,1280]{2,1,0:T(4,128)(2,1)S(1)} %slice.86), channel_id=1, source_target_pairs={{0,4},{4,8},{8,12},{12,16},{16,20},{20,24},{24,28},{28,0},{1,5},{5... | collective-permute-start | bytes 46088 | tf_op jit(solution)/shard_map/ppermute | solution.py:21
  70.8 3.1 %collective-permute-done.6 = bf16[2,3,1280]{2,1,0:T(4,128)(2,1)S(1)} collective-permute-done((bf16[2,3,1280]{2,1,0:T(4,128)(2,1)S(1)}, bf16[2,3,1280]{2,1,0:T(4,128)(2,1)S(1)}, u32[]{:S(2)}, u32[]{:S(2)}) %collective-permute-start.6) | collective-permute-done | bytes 15392 | tf_op jit(solution)/shard_map/ppermute | solution.py:21
  73.9 1.6 %maximum_convert_fusion = f32[2,259,1280]{2,1,0:T(8,128)S(1)} fusion(bf16[2,256,1280]{2,1,0:T(8,128)(2,1)} %bitcast.93, bf16[2,3,1280]{2,1,0:T(4,128)(2,1)S(1)} %fusion.14), kind=kLoop, calls=%fused_computation.19 | loop fusion | flops 2652160 | bytes 3978240 | tf_op jit(solution)/shard_map/convert_element_type | solution.py:284
  75.5 1.9 %multiply_convert_fusion = bf16[2,256,1280]{2,1,0:T(8,128)(2,1)S(1)} fusion(f32[2,259,1280]{2,1,0:T(8,128)S(1)} %maximum_convert_fusion, f32[1280]{0:T(1024)S(1)} %get-tuple-element.14, f32[1280]{0:T(1024)S(1)} %get-tuple-element.15, f32[1280]{0:T(1024)S(1)} %get-tuple-element.16, f32[1280]{0:T(1024)S(1)} %get-tuple-element.13, f32[1280]{0:T(1024)S(1)} %pad_maximum_fusion.9), kind=kLoop, calls=%fused_computation.11 | loop fusion | flops 8519680 | bytes 11822080 | tf_op jit(solution)/shard_map/convert_element_type | solution.py:288
  77.5 0.8 fusion.27
  78.2 1.6 %slice_convert_fusion = (f32[2,256,1024]{2,1,0:T(8,128)}, bf16[2,256,1024]{2,1,0:T(8,128)(2,1)S(1)}) fusion(bf16[2,256,1280]{2,1,0:T(8,128)(2,1)S(1)} %multiply_convert_fusion), kind=kLoop, calls=%fused_computation.85 | loop fusion | flops 524288 | bytes 4194304 | tf_op jit(solution)/shard_map/convert_element_type | solution.py:296
  79.8 2.9 %copy.62 = f32[2,256,1024]{1,2,0:T(8,128)} copy(f32[2,256,1024]{2,1,0:T(8,128)} %get-tuple-element.21) | data formatting | bytes 4194304 | tf_op jit(solution)/shard_map/convert_element_type | solution.py:296
  82.8 2.0 %convolution_convert_fusion.2 = bf16[2,16,64,128]{3,2,1,0:T(8,128)(2,1)S(1)} fusion(f32[2,256,16,64]{1,3,2,0:T(8,128)} %bitcast.91, f32[2,256,16]{1,2,0:T(8,128)} %get-tuple-element.28, bf16[2,256,1280]{2,1,0:T(8,128)(2,1)} %copy-done.5), kind=kOutput, calls=%fused_computation.21 | convolution fusion | flops 135528448 | bytes 2785280 | tf_op jit(solution)/shard_map/cqgjp,cqgn->cgjpn/dot_general | solution.py:297
  84.8 0.8 copy_bitcast_fusion.local_ref
  87.1 26.9 %exchange.1 = bf16[8,2,128,128]{3,2,1,0:T(8,128)(2,1)} custom-call(bf16[8,2,128,128]{3,2,1,0:T(8,128)(2,1)} %copy_bitcast_fusion.local_ref, f32[8,8,128]{2,1,0:T(8,128)} %broadcast_in_dim.28.grow_ref, f32[16,8,128]{2,1,0:T(8,128)} %broadcast_in_dim.29.pick_ref, f32[2,128,128]{2,1,0:T(8,128)} %constant_dynamic-slice_fusion.bank_ref), custom_call_target="tpu_custom_call" | custom-call | tf_op jit(solution)/shard_map/exchange/pallas_call | solution.py:110
  114.0 1.1 copy.67
  115.1 0.9 copy-done.1
  116.0 0.8 copy-done.2
  117.5 7.5 %finish.1 = bf16[2,256,1024]{2,1,0:T(8,128)(2,1)} custom-call(f32[2,256,16]{2,1,0:T(8,128)S(1)} %copy.68.cum_ref, f32[2,16,256]{2,1,0:T(8,128)S(1)} %copy-done.2, f32[2,16,256]{2,1,0:T(8,128)S(1)} %copy-done.3, bf16[2,256,1024]{2,1,0:T(8,128)(2,1)S(1)} %get-tuple-element.22.xs_ref, bf16[2,256,128]{2,1,0:T(8,128)(2,1)S(1)} %copy-done.1, ...), custom_call_target="tpu_custom_call" | custom-call | tf_op jit(solution)/shard_map/finish/pallas_call | solution.py:197
  (107 shorter events, 9.1 us)
Async XLA Ops:
  0.0 9.7 %copy-start = (f32[2,16,64,128]{3,2,1,0:T(8,128)S(1)}, f32[2,16,64,128]{3,2,1,0:T(8,128)}, u32[]{:S(2)}) copy-start(f32[2,16,64,128]{3,2,1,0:T(8,128)} %param.30) | copy-start | bytes 3145732
  0.0 1.6 %copy-start.7 = (bf16[512,1024]{1,0:T(8,128)(2,1)S(1)}, bf16[512,1024]{1,0:T(8,128)(2,1)}, u32[]{:S(2)}) copy-start(bf16[512,1024]{1,0:T(8,128)(2,1)} %param.18) | copy-start | bytes 3145732
  0.0 6.5 %copy-start.16 = (s32[3]{0:T(128)S(1)}, s32[3]{0:T(128)}, u32[]{:S(2)}) copy-start(s32[3]{0:T(128)} %param.33) | copy-start | bytes 40
  0.0 6.5 %copy-start.17 = (s32[3]{0:T(128)S(1)}, s32[3]{0:T(128)}, u32[]{:S(2)}) copy-start(s32[3]{0:T(128)} %param.34) | copy-start | bytes 40
  0.0 6.5 %copy-start.18 = (s32[3]{0:T(128)S(1)}, s32[3]{0:T(128)}, u32[]{:S(2)}) copy-start(s32[3]{0:T(128)} %param.35) | copy-start | bytes 40
  0.0 7.2 %copy-start.13 = (bf16[2,3,2,128]{3,2,1,0:T(2,128)(2,1)S(1)}, bf16[2,3,2,128]{3,2,1,0:T(2,128)(2,1)}, u32[]{:S(2)}) copy-start(bf16[2,3,2,128]{3,2,1,0:T(2,128)(2,1)} %param.32) | copy-start | bytes 9220
  0.0 7.3 %copy-start.10 = (f32[4,1024]{1,0:T(4,128)S(1)}, f32[4,1024]{1,0:T(4,128)}, u32[]{:S(2)}) copy-start(f32[4,1024]{1,0:T(4,128)} %param.22) | copy-start | bytes 49156
  2.9 6.8 %copy-start.11 = (f32[4,2,128]{2,1,0:T(2,128)S(1)}, f32[4,2,128]{2,1,0:T(2,128)}, u32[]{:S(2)}) copy-start(f32[4,2,128]{2,1,0:T(2,128)} %param.24) | copy-start | bytes 12292
  2.9 7.5 %copy-start.21 = (bf16[2,3,1024]{2,0,1:T(2,128)(2,1)S(1)}, bf16[2,3,1024]{2,0,1:T(2,128)(2,1)}, u32[]{:S(2)}) copy-start(bf16[2,3,1024]{2,0,1:T(2,128)(2,1)} %param.31) | copy-start | bytes 36868
  2.9 7.9 %copy-start.22 = (f32[16]{0:T(128)S(1)}, f32[16]{0:T(128)}, u32[]{:S(2)}) copy-start(f32[16]{0:T(128)} %param.26) | copy-start | bytes 196
  2.9 7.9 %copy-start.12 = (f32[1024]{0:T(1024)S(1)}, f32[1024]{0:T(1024)}, u32[]{:S(2)}) copy-start(f32[1024]{0:T(1024)} %param.23) | copy-start | bytes 12292
  2.9 7.9 %copy-start.15 = (f32[2,128]{1,0:T(2,128)S(1)}, f32[2,128]{1,0:T(2,128)}, u32[]{:S(2)}) copy-start(f32[2,128]{1,0:T(2,128)} %param.25) | copy-start | bytes 3076
  2.9 30.6 %collective-permute-start.4 = (bf16[256,1024]{1,0:T(8,128)(2,1)}, bf16[256,1024]{1,0:T(8,128)(2,1)S(1)}, u32[]{:S(2)}, u32[]{:S(2)}) collective-permute-start(bf16[256,1024]{1,0:T(8,128)(2,1)} %get-tuple-element.26), channel_id=1, source_target_pairs={{0,1},{1,0},{2,3},{3,2},{4,5},{5,4},{6,7},{7,6},{8,9},{9,8},{10,11... | collective-permute-start | bytes 1572872 | tf_op jit(solution)/shard_map/ppermute | solution.py:129
  3.5 24.6 %collective-permute-start.2 = (bf16[256,1024]{1,0:T(8,128)(2,1)}, bf16[256,1024]{1,0:T(8,128)(2,1)}, u32[]{:S(2)}, u32[]{:S(2)}) collective-permute-start(bf16[256,1024]{1,0:T(8,128)(2,1)} %get-tuple-element.26), channel_id=1, source_target_pairs={{0,2},{1,3},{2,0},{3,1},{4,6},{5,7},{6,4},{7,5},{8,10},{9,11},{10,... | collective-permute-start | bytes 1572872 | tf_op jit(solution)/shard_map/ppermute | solution.py:129
  6.0 24.8 %collective-permute-start = (bf16[256,1024]{1,0:T(8,128)(2,1)}, bf16[256,1024]{1,0:T(8,128)(2,1)}, u32[]{:S(2)}, u32[]{:S(2)}) collective-permute-start(bf16[256,1024]{1,0:T(8,128)(2,1)} %get-tuple-element.27), channel_id=1, source_target_pairs={{0,1},{1,0},{2,3},{3,2},{4,5},{5,4},{6,7},{7,6},{8,9},{9,8},{10,11... | collective-permute-start | bytes 1572872 | tf_op jit(solution)/shard_map/ppermute | solution.py:129
  6.2 23.8 %collective-permute-start.1 = (bf16[256,1024]{1,0:T(8,128)(2,1)}, bf16[256,1024]{1,0:T(8,128)(2,1)S(1)}, u32[]{:S(2)}, u32[]{:S(2)}) collective-permute-start(bf16[256,1024]{1,0:T(8,128)(2,1)} %get-tuple-element.27), channel_id=1, source_target_pairs={{0,2},{1,3},{2,0},{3,1},{4,6},{5,7},{6,4},{7,5},{8,10},{9,11},{10,... | collective-permute-start | bytes 1572872 | tf_op jit(solution)/shard_map/ppermute | solution.py:129
  10.9 19.3 %copy-start.19 = (f32[16]{0:T(128)S(1)}, f32[16]{0:T(128)}, u32[]{:S(2)}) copy-start(f32[16]{0:T(128)} %param.28) | copy-start | bytes 196
  30.0 6.4 %collective-permute-start.3 = (bf16[256,1024]{1,0:T(8,128)(2,1)S(1)}, bf16[256,1024]{1,0:T(8,128)(2,1)S(1)}, u32[]{:S(2)}, u32[]{:S(2)}) collective-permute-start(bf16[256,1024]{1,0:T(8,128)(2,1)S(1)} %collective-permute-done.1), channel_id=1, source_target_pairs={{0,1},{1,0},{2,3},{3,2},{4,5},{5,4},{6,7},{7,6},{8,9},{9,8},{10,11... | collective-permute-start | bytes 1572872 | tf_op jit(solution)/shard_map/ppermute | solution.py:129
  30.3 18.5 %collective-permute-start.5 = (bf16[256,1024]{1,0:T(8,128)(2,1)}, bf16[256,1024]{1,0:T(8,128)(2,1)S(1)}, u32[]{:S(2)}, u32[]{:S(2)}) collective-permute-start(bf16[256,1024]{1,0:T(8,128)(2,1)} %collective-permute-done.2), channel_id=1, source_target_pairs={{0,1},{1,0},{2,3},{3,2},{4,5},{5,4},{6,7},{7,6},{8,9},{9,8},{10,11... | collective-permute-start | bytes 1572872 | tf_op jit(solution)/shard_map/ppermute | solution.py:129
  36.4 13.2 %slice-start = ((s8[16777216]{0:T(1024)(128)(4,1)}), s8[4194304]{0:T(1024)(128)(4,1)S(1)}, s32[]{:S(2)}) async-start(s8[16777216]{0:T(1024)(128)(4,1)} %bitcast.88), calls=%async_computation | async-start | bytes 8388608
  37.3 12.4 %slice-start.1 = ((s8[16777216]{0:T(1024)(128)(4,1)}), s8[4194304]{0:T(1024)(128)(4,1)S(1)}, s32[]{:S(2)}) async-start(s8[16777216]{0:T(1024)(128)(4,1)} %bitcast.88), calls=%async_computation.1 | async-start | bytes 8388608
  37.3 12.4 %slice-start.2 = ((s8[16777216]{0:T(1024)(128)(4,1)}), s8[4194304]{0:T(1024)(128)(4,1)S(1)}, s32[]{:S(2)}) async-start(s8[16777216]{0:T(1024)(128)(4,1)} %bitcast.88), calls=%async_computation.2 | async-start | bytes 8388608
  37.3 12.4 %slice-start.3 = ((s8[16777216]{0:T(1024)(128)(4,1)}), s8[4194304]{0:T(1024)(128)(4,1)S(1)}, s32[]{:S(2)}) async-start(s8[16777216]{0:T(1024)(128)(4,1)} %bitcast.88), calls=%async_computation.3 | async-start | bytes 8388608
  49.7 7.3 %copy-start.20 = (bf16[4096,16]{0,1:T(8,128)(2,1)S(1)}, bf16[4096,16]{0,1:T(8,128)(2,1)}, u32[]{:S(2)}) copy-start(bf16[4096,16]{0,1:T(8,128)(2,1)} %param.21) | copy-start | bytes 393220
  57.0 3.4 %copy-start.14 = (f32[16]{0:T(128)S(1)}, f32[16]{0:T(128)}, u32[]{:S(2)}) copy-start(f32[16]{0:T(128)} %param.27) | copy-start | bytes 196
  62.7 4.2 %copy-start.8 = (bf16[256,2048]{1,0:T(8,128)(2,1)S(1)}, bf16[256,2048]{1,0:T(8,128)(2,1)}, u32[]{:S(2)}) copy-start(bf16[256,2048]{1,0:T(8,128)(2,1)} %convolution_convert_fusion) | copy-start | bytes 3145732
  67.2 1.8 %copy-start.6 = (bf16[512,1280]{1,0:T(8,128)(2,1)}, bf16[512,1280]{1,0:T(8,128)(2,1)S(1)}, u32[]{:S(2)}) copy-start(bf16[512,1280]{1,0:T(8,128)(2,1)S(1)} %pad_maximum_fusion.3) | copy-start | bytes 3932164
  67.3 6.6 %collective-permute-start.6 = (bf16[2,3,1280]{2,1,0:T(4,128)(2,1)S(1)}, bf16[2,3,1280]{2,1,0:T(4,128)(2,1)S(1)}, u32[]{:S(2)}, u32[]{:S(2)}) collective-permute-start(bf16[2,3,1280]{2,1,0:T(4,128)(2,1)S(1)} %slice.86), channel_id=1, source_target_pairs={{0,4},{4,8},{8,12},{12,16},{16,20},{20,24},{24,28},{28,0},{1,5},{5... | collective-permute-start | bytes 46088 | tf_op jit(solution)/shard_map/ppermute | solution.py:21
  77.4 2.4 %copy-start.5 = (bf16[2,256,1280]{2,1,0:T(8,128)(2,1)}, bf16[2,256,1280]{2,1,0:T(8,128)(2,1)S(1)}, u32[]{:S(2)}) copy-start(bf16[2,256,1280]{2,1,0:T(8,128)(2,1)S(1)} %multiply_convert_fusion) | copy-start | bytes 3932164
  82.8 3.6 %copy-start.9 = (f32[8,8]{1,0:T(8,128)S(1)}, f32[8,8]{1,0:T(8,128)}, u32[]{:S(2)}) copy-start(f32[8,8]{1,0:T(8,128)} %pad.9.clone) | copy-start | bytes 772
  84.8 30.2 %copy-start.4 = (f32[1024]{0:T(1024)S(1)}, f32[1024]{0:T(1024)}, u32[]{:S(2)}) copy-start(f32[1024]{0:T(1024)} %param.29) | copy-start | bytes 12292
  115.1 0.9 copy-start.1
  (2 other events, 1.5 us)

commit v3 on v2

--- a/solution.py
+++ b/solution.py
@@ -137,13 +137,59 @@
     near = [swap(part, axis, 1) for part in own]
     far, weights = lax.optimization_barrier((far, weights))
     both = [swap(part, axis, 1) for part in far]
-    wholes = []
-    for parts in zip(own, near, far, both):
-        whole = jnp.zeros((BLOCK, width * 4), hidden.dtype)
-        for bits, part in enumerate(parts):
-            whole = lax.dynamic_update_slice_in_dim(whole, part, (mine ^ bits) * width, axis=1)
-        wholes.append(whole)
-    return wholes, weights
+    return [part for parts in (own, near, far, both) for part in parts], weights
+
+
+def project_kernel(blocks, *refs):
+    parts, (zx_w, bc_w, dt_w, zx_ref, bc_ref, dt_ref) = refs[: 4 * blocks], refs[4 * blocks :]
+    mine, width = lax.axis_index("mp"), parts[0].shape[1]
+
+    def product(weight_ref):
+        total = None
+        for bits in range(4):
+            rows = [part[...] for part in parts[bits * blocks : (bits + 1) * blocks]]
+            at = pl.multiple_of((mine ^ bits) * width, width)
+            term = jnp.dot(
+                jnp.concatenate(rows, axis=0),
+                weight_ref[pl.ds(at, width), :],
+                preferred_element_type=jnp.float32,
+            )
+            total = term if total is None else total + term
+        return total
+
+    zx_ref[...] = product(zx_w).astype(jnp.bfloat16)
+
+    @pl.when(pl.program_id(0) == 0)
+    def _():
+        bc_ref[...] = product(bc_w).astype(jnp.bfloat16)
+        dt_ref[...] = product(dt_w)
+
+
+def project(parts, zx_w, bc_w, dt_w):
+    blocks, tile = len(parts) // 4, 512
+    rows = blocks * BLOCK
+
+    def fixed(shape):
+        return pl.BlockSpec(shape, lambda n: (0, 0))
+
+    return pl.pallas_call(
+        functools.partial(project_kernel, blocks),
+        grid=(zx_w.shape[1] // tile,),
+        out_shape=(
+            jax.ShapeDtypeStruct((rows, zx_w.shape[1]), jnp.bfloat16),
+            jax.ShapeDtypeStruct((rows, bc_w.shape[1]), jnp.bfloat16),
+            jax.ShapeDtypeStruct((rows, dt_w.shape[1]), jnp.float32),
+        ),
+        in_specs=[fixed(part.shape) for part in parts]
+        + [pl.BlockSpec((WIDTH, tile), lambda n: (0, n)), fixed(bc_w.shape), fixed(dt_w.shape)],
+        out_specs=(
+            pl.BlockSpec((rows, tile), lambda n: (0, n)),
+            fixed((rows, bc_w.shape[1])),
+            fixed((rows, dt_w.shape[1])),
+        ),
+        compiler_params=pltpu.CompilerParams(vmem_limit_bytes=40 * 1024 * 1024),
+        name="project",
+    )(*parts, zx_w, bc_w, dt_w)
 
 
 def tail_kernel(
@@ -240,13 +286,7 @@
     flat_zx = w_zx.reshape(WIDTH, 2 * inner_dev)
     flat_bc = w_bc.reshape(WIDTH, 2 * gstate_dev)
     pieces, flat_zx = gather_columns(hidden, "mp", flat_zx)
-    zx = [
-        jnp.dot(piece, flat_zx, preferred_element_type=jnp.float32).astype(jnp.bfloat16)
-        for piece in pieces
-    ]
-    zx, piece = jnp.concatenate(zx, axis=0), jnp.concatenate(pieces, axis=0)
-    bc = jnp.dot(piece, flat_bc, preferred_element_type=jnp.float32).astype(jnp.bfloat16)
-    dt_raw = jnp.dot(piece, w_dt, preferred_element_type=jnp.float32)
+    zx, bc, dt_raw = project(pieces, flat_zx, flat_bc, w_dt)
     gate = zx[:, :inner_dev]
     mixin = jnp.concatenate([zx[:, inner_dev:], bc], axis=1).reshape(blocks, BLOCK, channels)
     own_tails = mixin[:, BLOCK - (KERNEL - 1) :, :]

time: 126 us -> 109 us (0.87)
  matrix products: 28.6 us -> 2.27 us
  Pallas kernels: 34.4 us -> 49.6 us
  local copies, waits for them, and re-layouts: 41.6 us -> 36 us
  waiting for transfers between devices: 5.05 us -> 3.48 us
    dot_general x4 -> x0, matrix products: 26.4 us -> none  [the longest x2 18.8 us: per_device(): jnp.dot(piece, flat_zx, preferred_element_type=jnp.float32)]
    pallas_call x0 -> x1, Pallas kernels: none -> 15 us  [project(): pl.pallas_call(functools.partial(project_kernel, blocks), grid=(zx_w.shap...]
    dynamic_update_slice x8 -> x0, local copies, waits for them, and re-layouts: 9.48 us -> none  [gather_columns(): lax.dynamic_update_slice_in_dim(whole, part, (mine ^ bits) * width, axis=1)]
    unnamed x59 -> x47, local copies, waits for them, and re-layouts: 19.8 us -> 24.3 us
    another operation x4 -> x2, local copies, waits for them, and re-layouts: 3.25 us -> 0.13 us
    slice x1 -> x3, local copies, waits for them, and re-layouts: 0.16 us -> 2.69 us  [the longest x1 2.35 us: gather_columns(): own = [hidden[start:start + BLOCK] for start in starts]]
    ppermute x1, waiting for transfers between devices: 3.08 us -> 0.65 us  [from_behind(): return lax.ppermute(value, axis, pairs)]
  transfers between devices with their start and end apart: 7 -> 7, of which waited for: 2 -> 4; matrix products, arithmetic and copies ran while one was open for 33% -> 24% of each run, Pallas kernels for 0% -> 0%
where the time goes in v3:
time: 109 us; the launch traced here: 107 us
  Pallas kernels  49.6 us (46%)
  local copies, waits for them, and re-layouts  36 us (33%)
  other arithmetic  9.62 us (9%)
  starting transfers between devices  5.94 us (5%)
  waiting for transfers between devices  3.48 us (3%)
  matrix products  2.27 us (2%)
    pallas_call x1, Pallas kernels, entering_states(): pl.pallas_call(functools.partial(exchange_kernel, count, blocks), out_sha...  27.1 us
    unnamed x47, local copies, waits for them, and re-layouts  24.3 us
    pallas_call x1, Pallas kernels, project(): pl.pallas_call(functools.partial(project_kernel, blocks), grid=(zx_w.shap...  15 us
    pallas_call x1, Pallas kernels, finish(): pl.pallas_call(functools.partial(tail_kernel, per_group), grid=(blocks,),...  7.52 us
    ppermute x6, starting transfers between devices, swap(): lax.ppermute(value, axis, [(source, source ^ bit) for source in range(cou...  3.99 us
    convert_element_type x1, local copies, waits for them, and re-layouts, per_device(): weighted = (xs.astype(jnp.float32) * factor).astype(jnp.bfloat16)  2.89 us
    ppermute x6, waiting for transfers between devices, swap(): lax.ppermute(value, axis, [(source, source ^ bit) for source in range(cou...  2.83 us
    slice x1, local copies, waits for them, and re-layouts, gather_columns(): own = [hidden[start:start + BLOCK] for start in starts]  2.35 us
  transfers between devices with their start and end apart: 7, of which 4 were waited for; matrix products, arithmetic and copies ran while one was open for 24% of the time, Pallas kernels for 0%

profile of v3, /device:TPU:0, one launch (start us, length us, event | category | flops | bytes accessed | tf_op | source)
XLA Modules:
  0.0 107.2 jit_solution(3154205579280604465)
XLA Ops:
  0.0 2.3 %fusion.19 = (bf16[256,1024]{1,0:T(8,128)(2,1)}, bf16[256,1024]{1,0:T(8,128)(2,1)}) fusion(bf16[512,1024]{1,0:T(8,128)(2,1)} %param.18), kind=kLoop, calls=%fused_computation.66 | loop fusion | bytes 2097152 | tf_op jit(solution)/shard_map/slice | solution.py:135
  2.4 3.0 %collective-permute-start.2 = (bf16[256,1024]{1,0:T(8,128)(2,1)}, bf16[256,1024]{1,0:T(8,128)(2,1)}, u32[]{:S(2)}, u32[]{:S(2)}) collective-permute-start(bf16[256,1024]{1,0:T(8,128)(2,1)} %get-tuple-element.32.refs_0_), channel_id=1, source_target_pairs={{0,2},{1,3},{2,0},{3,1},{4,6},{5,7},{6,4},{7,5},{8,10},{9,11},{10,... | collective-permute-start | bytes 1572872 | tf_op jit(solution)/shard_map/ppermute | solution.py:129
  5.8 0.9 select_reduce_fusion.2
  7.0 17.3 %copy.79 = bf16[512,8,2,1024]{3,1,2,0:T(8,128)(2,1)} copy(bf16[512,8,2,1024]{3,2,1,0:T(2,128)(2,1)} %bitcast.71) | data formatting | bytes 33554432
  25.2 1.3 %copy.58.refs_10_ = bf16[4096,16]{1,0:T(8,128)(2,1)} copy(bf16[4096,16]{0,1:T(8,128)(2,1)S(1)} %copy-done.9) | data formatting | bytes 262144 | tf_op args[3]
  27.3 0.7 constant_dynamic-slice_fusion.bank_ref
  28.1 0.7 collective-permute-done.3.refs_5_
  29.6 1.3 %collective-permute-done.4.refs_6_ = bf16[256,1024]{1,0:T(8,128)(2,1)S(1)} collective-permute-done((bf16[256,1024]{1,0:T(8,128)(2,1)}, bf16[256,1024]{1,0:T(8,128)(2,1)S(1)}, u32[]{:S(2)}, u32[]{:S(2)}) %collective-permute-start.4) | collective-permute-done | bytes 524320 | tf_op jit(solution)/shard_map/ppermute | solution.py:129
  30.9 0.7 collective-permute-done.5.refs_7_
  31.7 1.2 %copy-done.1 = bf16[4096,16]{1,0:T(8,128)(2,1)S(1)} copy-done((bf16[4096,16]{1,0:T(8,128)(2,1)S(1)}, bf16[4096,16]{1,0:T(8,128)(2,1)}, u32[]{:S(2)}) %copy-start.1) | copy-done | bytes 131096
  32.9 15.0 %project.1 = (bf16[512,2048]{1,0:T(8,128)(2,1)S(1)}, bf16[512,256]{1,0:T(8,128)(2,1)S(1)}, f32[512,16]{1,0:T(8,128)S(1)}) custom-call(bf16[256,1024]{1,0:T(8,128)(2,1)} %get-tuple-element.32.refs_0_, bf16[256,1024]{1,0:T(8,128)(2,1)} %get-tuple-element.31.refs_1_, bf16[256,1024]{1,0:T(8,128)(2,1)} %collective-permute-done.refs_2_, ...), custom_call_target="tpu_custom_call" | custom-call | tf_op jit(solution)/shard_map/project/pallas_call | solution.py:175
  48.2 1.1 copy-done.7
  49.3 1.9 %collective-permute-start.6 = (bf16[2,3,1280]{2,1,0:T(4,128)(2,1)S(1)}, bf16[2,3,1280]{2,1,0:T(4,128)(2,1)S(1)}, u32[]{:S(2)}, u32[]{:S(2)}) collective-permute-start(bf16[2,3,1280]{2,1,0:T(4,128)(2,1)S(1)} %slice.84), channel_id=1, source_target_pairs={{0,4},{4,8},{8,12},{12,16},{16,20},{20,24},{24,28},{28,0},{1,5},{5... | collective-permute-start | bytes 46088 | tf_op jit(solution)/shard_map/ppermute | solution.py:21
  51.4 1.2 %reduce-window.14 = f32[2,16,2,128]{3,1,2,0:T(8,128)S(1)} reduce-window(f32[2,16,2,128]{3,1,2,0:T(8,128)S(1)} %copy_bitcast_fusion.3, f32[]{:T(128)} %constant.26.clone.1), window={size=1x1x1x128 pad=0_0x0_0x0_0x127_0}, to_apply=%region_0.1 | reduce-window | flops 1040384 | bytes 65540 | tf_op jit(solution)/shard_map/reduce-window
  52.8 0.7 copy_bitcast_fusion.2
  53.7 0.7 exponential_multiply_fusion
  55.4 0.6 collective-permute-done.6
  56.1 1.6 %maximum_convert_fusion = f32[2,259,1280]{2,1,0:T(8,128)S(1)} fusion(bf16[2,256,1280]{2,1,0:T(8,128)(2,1)} %bitcast.74, bf16[2,3,1280]{2,1,0:T(4,128)(2,1)S(1)} %fusion.6), kind=kLoop, calls=%fused_computation.11 | loop fusion | flops 2652160 | bytes 3978240 | tf_op jit(solution)/shard_map/convert_element_type | solution.py:324
  57.7 1.7 %multiply_convert_fusion = bf16[2,256,1280]{2,1,0:T(8,128)(2,1)S(1)} fusion(f32[2,259,1280]{2,1,0:T(8,128)S(1)} %maximum_convert_fusion, f32[1280]{0:T(1024)S(1)} %get-tuple-element.20, f32[1280]{0:T(1024)S(1)} %get-tuple-element.21, f32[1280]{0:T(1024)S(1)} %get-tuple-element.22, f32[1280]{0:T(1024)S(1)} %get-tuple-element.19, f32[1280]{0:T(1024)S(1)} %pad_maximum_fusion.3), kind=kLoop, calls=%fused_computation.8 | loop fusion | flops 8519680 | bytes 11822080 | tf_op jit(solution)/shard_map/convert_element_type | solution.py:328
  59.5 1.7 %slice_convert_fusion = (f32[2,256,1024]{2,1,0:T(8,128)}, bf16[2,256,1024]{2,1,0:T(8,128)(2,1)S(1)}) fusion(bf16[2,256,1280]{2,1,0:T(8,128)(2,1)S(1)} %multiply_convert_fusion), kind=kLoop, calls=%fused_computation.63 | loop fusion | flops 524288 | bytes 4194304 | tf_op jit(solution)/shard_map/convert_element_type | solution.py:336
  61.2 0.7 fusion.18
  61.9 2.9 %copy.65 = f32[2,256,1024]{1,2,0:T(8,128)} copy(f32[2,256,1024]{2,1,0:T(8,128)} %get-tuple-element.27) | data formatting | bytes 4194304 | tf_op jit(solution)/shard_map/convert_element_type | solution.py:336
  64.8 2.1 %convolution_convert_fusion = bf16[2,16,64,128]{3,2,1,0:T(8,128)(2,1)S(1)} fusion(f32[2,256,16,64]{1,3,2,0:T(8,128)} %bitcast.72, f32[2,256,16]{1,2,0:T(8,128)} %get-tuple-element.33, bf16[2,256,1280]{2,1,0:T(8,128)(2,1)} %copy-done.6), kind=kOutput, calls=%fused_computation.13 | convolution fusion | flops 135528448 | bytes 2785280 | tf_op jit(solution)/shard_map/cqgjp,cqgn->cgjpn/dot_general | solution.py:337
  66.9 0.8 copy_bitcast_fusion.1.local_ref
  67.7 0.7 broadcast_in_dim.28.grow_ref
  68.4 0.7 broadcast_in_dim.29.pick_ref
  69.1 27.1 %exchange.1 = bf16[8,2,128,128]{3,2,1,0:T(8,128)(2,1)} custom-call(bf16[8,2,128,128]{3,2,1,0:T(8,128)(2,1)} %copy_bitcast_fusion.1.local_ref, f32[8,8,128]{2,1,0:T(8,128)} %broadcast_in_dim.28.grow_ref, f32[16,8,128]{2,1,0:T(8,128)} %broadcast_in_dim.29.pick_ref, f32[2,128,128]{2,1,0:T(8,128)} %constant_dynamic-slice_fusion.bank_ref), custom_call_target="tpu_custom_call" | custom-call | tf_op jit(solution)/shard_map/exchange/pallas_call | solution.py:110
  96.2 1.1 %copy.70 = bf16[2,8,128,128]{3,2,1,0:T(8,128)(2,1)S(1)} copy(bf16[2,8,128,128]{3,2,0,1:T(8,128)(2,1)} %bitcast.76) | data formatting | bytes 1048576 | tf_op jit(solution)/shard_map/transpose | solution.py:124
  97.3 0.9 copy-done.2
  98.2 0.8 copy-done.3
  98.9 0.8 copy-done.4
  99.7 7.5 %finish.1 = bf16[2,256,1024]{2,1,0:T(8,128)(2,1)} custom-call(f32[2,256,16]{2,1,0:T(8,128)S(1)} %copy.71.cum_ref, f32[2,16,256]{2,1,0:T(8,128)S(1)} %copy-done.3, f32[2,16,256]{2,1,0:T(8,128)S(1)} %copy-done.4, bf16[2,256,1024]{2,1,0:T(8,128)(2,1)S(1)} %get-tuple-element.28.xs_ref, bf16[2,256,128]{2,1,0:T(8,128)(2,1)S(1)} %copy-done.2, ...), custom_call_target="tpu_custom_call" | custom-call | tf_op jit(solution)/shard_map/finish/pallas_call | solution.py:243
  (83 shorter events, 5.1 us)
Async XLA Ops:
  0.0 27.3 %copy-start = (f32[2,16,64,128]{3,2,1,0:T(8,128)S(1)}, f32[2,16,64,128]{3,2,1,0:T(8,128)}, u32[]{:S(2)}) copy-start(f32[2,16,64,128]{3,2,1,0:T(8,128)} %param.30) | copy-start | bytes 3145732
  2.4 25.7 %collective-permute-start.2 = (bf16[256,1024]{1,0:T(8,128)(2,1)}, bf16[256,1024]{1,0:T(8,128)(2,1)}, u32[]{:S(2)}, u32[]{:S(2)}) collective-permute-start(bf16[256,1024]{1,0:T(8,128)(2,1)} %get-tuple-element.32.refs_0_), channel_id=1, source_target_pairs={{0,2},{1,3},{2,0},{3,1},{4,6},{5,7},{6,4},{7,5},{8,10},{9,11},{10,... | collective-permute-start | bytes 1572872 | tf_op jit(solution)/shard_map/ppermute | solution.py:129
  5.3 24.2 %collective-permute-start = (bf16[256,1024]{1,0:T(8,128)(2,1)}, bf16[256,1024]{1,0:T(8,128)(2,1)}, u32[]{:S(2)}, u32[]{:S(2)}) collective-permute-start(bf16[256,1024]{1,0:T(8,128)(2,1)} %get-tuple-element.32.refs_0_), channel_id=1, source_target_pairs={{0,1},{1,0},{2,3},{3,2},{4,5},{5,4},{6,7},{7,6},{8,9},{9,8},{10,11... | collective-permute-start | bytes 1572872 | tf_op jit(solution)/shard_map/ppermute | solution.py:129
  5.3 23.5 %collective-permute-start.3 = (bf16[256,1024]{1,0:T(8,128)(2,1)}, bf16[256,1024]{1,0:T(8,128)(2,1)}, u32[]{:S(2)}, u32[]{:S(2)}) collective-permute-start(bf16[256,1024]{1,0:T(8,128)(2,1)} %get-tuple-element.31.refs_1_), channel_id=1, source_target_pairs={{0,2},{1,3},{2,0},{3,1},{4,6},{5,7},{6,4},{7,5},{8,10},{9,11},{10,... | collective-permute-start | bytes 1572872 | tf_op jit(solution)/shard_map/ppermute | solution.py:129
  5.4 24.2 %collective-permute-start.1 = (bf16[256,1024]{1,0:T(8,128)(2,1)}, bf16[256,1024]{1,0:T(8,128)(2,1)}, u32[]{:S(2)}, u32[]{:S(2)}) collective-permute-start(bf16[256,1024]{1,0:T(8,128)(2,1)} %get-tuple-element.31.refs_1_), channel_id=1, source_target_pairs={{0,1},{1,0},{2,3},{3,2},{4,5},{5,4},{6,7},{7,6},{8,9},{9,8},{10,11... | collective-permute-start | bytes 1572872 | tf_op jit(solution)/shard_map/ppermute | solution.py:129
  7.0 17.3 %copy-start.8 = (bf16[4096,2,128]{2,1,0:T(2,128)(2,1)S(1)}, bf16[4096,2,128]{2,1,0:T(2,128)(2,1)}, u32[]{:S(2)}) copy-start(bf16[4096,2,128]{2,1,0:T(2,128)(2,1)} %param.20) | copy-start | bytes 6291460
  24.3 0.9 copy-start.9
  24.3 2.7 %copy-start.14 = (bf16[2,3,2,128]{3,2,1,0:T(2,128)(2,1)S(1)}, bf16[2,3,2,128]{3,2,1,0:T(2,128)(2,1)}, u32[]{:S(2)}) copy-start(bf16[2,3,2,128]{3,2,1,0:T(2,128)(2,1)} %param.32) | copy-start | bytes 9220
  24.3 2.8 %copy-start.17 = (f32[16]{0:T(128)S(1)}, f32[16]{0:T(128)}, u32[]{:S(2)}) copy-start(f32[16]{0:T(128)} %param.28) | copy-start | bytes 196
  24.3 3.0 %copy-start.11 = (f32[4,1024]{1,0:T(4,128)S(1)}, f32[4,1024]{1,0:T(4,128)}, u32[]{:S(2)}) copy-start(f32[4,1024]{1,0:T(4,128)} %param.22) | copy-start | bytes 49156
  24.3 3.6 %copy-start.12 = (f32[4,2,128]{2,1,0:T(2,128)S(1)}, f32[4,2,128]{2,1,0:T(2,128)}, u32[]{:S(2)}) copy-start(f32[4,2,128]{2,1,0:T(2,128)} %param.24) | copy-start | bytes 12292
  24.3 5.0 %copy-start.13 = (f32[1024]{0:T(1024)S(1)}, f32[1024]{0:T(1024)}, u32[]{:S(2)}) copy-start(f32[1024]{0:T(1024)} %param.23) | copy-start | bytes 12292
  24.4 5.0 %copy-start.16 = (f32[2,128]{1,0:T(2,128)S(1)}, f32[2,128]{1,0:T(2,128)}, u32[]{:S(2)}) copy-start(f32[2,128]{1,0:T(2,128)} %param.25) | copy-start | bytes 3076
  24.4 5.0 %copy-start.19 = (f32[16]{0:T(128)S(1)}, f32[16]{0:T(128)}, u32[]{:S(2)}) copy-start(f32[16]{0:T(128)} %param.26) | copy-start | bytes 196
  24.4 5.0 %copy-start.18 = (bf16[2,3,1024]{2,0,1:T(2,128)(2,1)S(1)}, bf16[2,3,1024]{2,0,1:T(2,128)(2,1)}, u32[]{:S(2)}) copy-start(bf16[2,3,1024]{2,0,1:T(2,128)(2,1)} %param.31) | copy-start | bytes 36868
  28.8 2.1 %collective-permute-start.4 = (bf16[256,1024]{1,0:T(8,128)(2,1)}, bf16[256,1024]{1,0:T(8,128)(2,1)S(1)}, u32[]{:S(2)}, u32[]{:S(2)}) collective-permute-start(bf16[256,1024]{1,0:T(8,128)(2,1)} %collective-permute-done.2.refs_4_), channel_id=1, source_target_pairs={{0,1},{1,0},{2,3},{3,2},{4,5},{5,4},{6,7},{7,6},{8,9},{9,8},{10,11... | collective-permute-start | bytes 1572872 | tf_op jit(solution)/shard_map/ppermute | solution.py:129
  28.8 2.9 %collective-permute-start.5 = (bf16[256,1024]{1,0:T(8,128)(2,1)}, bf16[256,1024]{1,0:T(8,128)(2,1)S(1)}, u32[]{:S(2)}, u32[]{:S(2)}) collective-permute-start(bf16[256,1024]{1,0:T(8,128)(2,1)} %collective-permute-done.3.refs_5_), channel_id=1, source_target_pairs={{0,1},{1,0},{2,3},{3,2},{4,5},{5,4},{6,7},{7,6},{8,9},{9,8},{10,11... | collective-permute-start | bytes 1572872 | tf_op jit(solution)/shard_map/ppermute | solution.py:129
  31.7 1.2 %copy-start.1 = (bf16[4096,16]{1,0:T(8,128)(2,1)S(1)}, bf16[4096,16]{1,0:T(8,128)(2,1)}, u32[]{:S(2)}) copy-start(bf16[4096,16]{1,0:T(8,128)(2,1)} %copy.58.refs_10_) | copy-start | bytes 393220
  47.9 3.4 %copy-start.15 = (f32[16]{0:T(128)S(1)}, f32[16]{0:T(128)}, u32[]{:S(2)}) copy-start(f32[16]{0:T(128)} %param.27) | copy-start | bytes 196
  48.2 1.1 copy-start.7
  49.3 6.7 %collective-permute-start.6 = (bf16[2,3,1280]{2,1,0:T(4,128)(2,1)S(1)}, bf16[2,3,1280]{2,1,0:T(4,128)(2,1)S(1)}, u32[]{:S(2)}, u32[]{:S(2)}) collective-permute-start(bf16[2,3,1280]{2,1,0:T(4,128)(2,1)S(1)} %slice.84), channel_id=1, source_target_pairs={{0,4},{4,8},{8,12},{12,16},{16,20},{20,24},{24,28},{28,0},{1,5},{5... | collective-permute-start | bytes 46088 | tf_op jit(solution)/shard_map/ppermute | solution.py:21
  59.5 1.7 %copy-start.6 = (bf16[2,256,1280]{2,1,0:T(8,128)(2,1)}, bf16[2,256,1280]{2,1,0:T(8,128)(2,1)S(1)}, u32[]{:S(2)}) copy-start(bf16[2,256,1280]{2,1,0:T(8,128)(2,1)S(1)} %multiply_convert_fusion) | copy-start | bytes 3932164
  64.8 2.9 %copy-start.10 = (f32[8,8]{1,0:T(8,128)S(1)}, f32[8,8]{1,0:T(8,128)}, u32[]{:S(2)}) copy-start(f32[8,8]{1,0:T(8,128)} %pad.9.clone) | copy-start | bytes 772
  64.8 32.4 %copy-start.5 = (f32[1024]{0:T(1024)S(1)}, f32[1024]{0:T(1024)}, u32[]{:S(2)}) copy-start(f32[1024]{0:T(1024)} %param.29) | copy-start | bytes 12292
  97.3 0.9 copy-start.2
  98.2 0.8 copy-start.3
  98.9 0.8 copy-start.4
